TPU v7x, 32 devices: a whole 2x2x4 slice. The times are simulated.
32 devices in a mesh: replica: 8 (over z, y), weight: 4 (over x, core).
Axes of the slice: x: 2, y: 2, z: 4, core: 2. Of those that a mesh axis runs over, the one named last changes fastest.
Arguments:
- images: bfloat16 [512, 14, 14, 512], P(('replica', 'weight')), may hold values from -6 to 6
- gains: bfloat16 [2, 512], P(None, 'weight'), may hold values from 0.5 to 1.5
- biases: bfloat16 [6, 512], P(None, 'weight'), may hold values from -2 to 2
- qkv_weight: bfloat16 [512, 1536], P('weight'), may hold values from -0.25 to 0.25
- bias_table: bfloat16 [169, 16], P(None, 'weight'), may hold values from -4 to 4
- proj_weight: bfloat16 [512, 512], P('weight'), may hold values from -2 to 2
- fc1_weight: bfloat16 [512, 2048], P('weight'), may hold values from -0.25 to 0.25
- fc1_bias: bfloat16 [2048], P('weight'), may hold values from -2 to 2
- fc2_weight: bfloat16 [2048, 512], P('weight'), may hold values from -0.125 to 0.125
- rel_index: int32 [49, 49], replicated, may hold values from 0 to 168, as said below
- cotangent: bfloat16 [512, 14, 14, 512], P(('replica', 'weight')), may hold values from -6 to 6
Outputs:
- output: bfloat16 [512, 14, 14, 512], P(('replica', 'weight'))
- input_grad: bfloat16 [512, 14, 14, 512], P(('replica', 'weight'))
- gains_grad: float32 [2, 512], P(None, 'weight')
- biases_grad: float32 [6, 512], P(None, 'weight')
- qkv_grad: float32 [512, 1536], P('weight')
- table_grad: float32 [169, 16], P(None, 'weight')
- proj_grad: float32 [512, 512], P('weight')
- fc1_grad: float32 [512, 2048], P('weight')
- fc1_bias_grad: float32 [2048], P('weight')
- fc2_grad: float32 [2048, 512], P('weight')
Inputs may be any that keep to these rules, and one draw needn't show every extreme that they name: `rel_index`: entries of two query and key pairs hold the same value exactly when the pairs have the same relative offset within a window; all (7*2-1)^2 values occur.
All inputs are finite; a program needn't handle non-finite values.
Results may differ from a plain program's by a relative error of at most 0.013.
Values may be sent and summed in bfloat16 or wider, within the bound.
A program may use at most 320 MiB of HBM per device.

v0:
```python
import jax
import jax.numpy as jnp
from jax import lax
from jax.sharding import PartitionSpec as P

GRID = 14
WIN = 7
SHIFT = 3


epsilon = 1e-05
highest = lax.Precision.HIGHEST


def layer_norm(values, gain, offset):
    center = values - jnp.mean(values, axis=-1, keepdims=True)
    spread = jnp.mean(center * center, axis=-1, keepdims=True)
    return center * lax.rsqrt(spread + epsilon) * gain + offset


def exact_gelu(values):
    return jax.nn.gelu(values, approximate=False)


def to_windows(pictures):
    number = pictures.shape[0]
    across = GRID // WIN
    tiles = pictures.reshape(number, across, WIN, across, WIN, pictures.shape[-1])
    return tiles.transpose(0, 1, 3, 2, 4, 5).reshape(
        number * across * across, WIN * WIN, pictures.shape[-1]
    )


def from_windows(windows):
    across = GRID // WIN
    number = windows.shape[0] // (across * across)
    tiles = windows.reshape(number, across, across, WIN, WIN, windows.shape[-1])
    return tiles.transpose(0, 1, 3, 2, 4, 5).reshape(number, GRID, GRID, windows.shape[-1])


def region_mask():
    places = jnp.arange(GRID, dtype=jnp.int32)
    bands = (places >= GRID - WIN).astype(jnp.int32) + (places >= GRID - SHIFT).astype(jnp.int32)
    labels = bands[:, None] * 3 + bands[None, :]
    across = GRID // WIN
    labels = (
        labels.reshape(across, WIN, across, WIN)
        .transpose(0, 2, 1, 3)
        .reshape(across * across, WIN * WIN)
    )
    return jnp.where(labels[:, :, None] == labels[:, None, :], 0.0, -100.0).astype(jnp.float32)


def one_hot_index(rel_index):
    entries = jnp.arange((2 * WIN - 1) ** 2, dtype=jnp.int32)
    return (rel_index.reshape(-1)[:, None] == entries[None, :]).astype(jnp.float32)


def attention_scores(queries, keys_all, rel_bias, mask_tiled, scale):
    raw_scores = jnp.einsum(
        "wqhe,wkhe->whqk", queries, keys_all, preferred_element_type=jnp.float32
    )
    return scale * raw_scores + rel_bias[None] + mask_tiled[:, None]


def per_device(
    images,
    gains,
    biases,
    qkv_weight,
    bias_table,
    proj_weight,
    fc1_weight,
    fc1_bias,
    fc2_weight,
    rel_index,
    cotangent,
):
    gathered = (
        lax.all_gather(gains, "weight", axis=1, tiled=True),
        lax.all_gather(biases, "weight", axis=1, tiled=True),
        lax.all_gather(qkv_weight, "weight", axis=0, tiled=True),
        lax.all_gather(bias_table, "weight", axis=1, tiled=True),
        lax.all_gather(proj_weight, "weight", axis=0, tiled=True),
        lax.all_gather(fc1_weight, "weight", axis=0, tiled=True),
        lax.all_gather(fc1_bias, "weight", axis=0, tiled=True),
        lax.all_gather(fc2_weight, "weight", axis=0, tiled=True),
    )
    (
        full_gains,
        full_biases,
        full_qkv,
        full_table,
        full_proj,
        full_expand,
        full_expand_bias,
        full_reduce,
    ) = gathered
    gains_float = full_gains.astype(jnp.float32)
    biases_float = full_biases.astype(jnp.float32)
    number = images.shape[0]
    width = images.shape[-1]
    heads = full_table.shape[1]
    size_head = width // heads
    scale = size_head ** (-0.5)
    window_in = to_windows(jnp.roll(images, (-SHIFT, -SHIFT), (1, 2)).astype(jnp.float32))
    windows = window_in.shape[0]
    length = window_in.shape[1]
    flat_in = window_in.reshape(-1, width)
    mask_tiled = jnp.tile(region_mask(), (number, 1, 1))
    table_hot = one_hot_index(rel_index)
    rel_bias = (
        jnp.dot(table_hot, full_table.astype(jnp.float32), precision=highest)
        .reshape(length, length, heads)
        .transpose(2, 0, 1)
    )
    normed_low = layer_norm(flat_in, gains_float[0], biases_float[0]).astype(jnp.bfloat16)
    qkv_bias = jnp.concatenate([biases_float[2], jnp.zeros_like(biases_float[2]), biases_float[3]])
    mixed = (jnp.dot(normed_low, full_qkv, preferred_element_type=jnp.float32) + qkv_bias).astype(
        jnp.bfloat16
    )
    mixed = mixed.reshape(windows, length, 3, heads, size_head)
    queries = mixed[:, :, 0]
    keys_all = mixed[:, :, 1]
    values_all = mixed[:, :, 2]
    scores = attention_scores(queries, keys_all, rel_bias, mask_tiled, scale)
    top_score = jnp.max(scores, axis=-1, keepdims=True)
    log_total = top_score + jnp.log(jnp.sum(jnp.exp(scores - top_score), axis=-1, keepdims=True))
    probs_low = jnp.exp(scores - log_total).astype(jnp.bfloat16)
    attended = jnp.einsum(
        "whqk,wkhe->wqhe", probs_low, values_all, preferred_element_type=jnp.float32
    )
    attended = attended.reshape(-1, width).astype(jnp.bfloat16)
    middle = (
        flat_in + jnp.dot(attended, full_proj, preferred_element_type=jnp.float32) + biases_float[4]
    )
    normed_two = layer_norm(middle, gains_float[1], biases_float[1]).astype(jnp.bfloat16)
    hidden = jnp.dot(
        normed_two, full_expand, preferred_element_type=jnp.float32
    ) + full_expand_bias.astype(jnp.float32)
    activated = exact_gelu(hidden).astype(jnp.bfloat16)
    final = (
        middle
        + jnp.dot(activated, full_reduce, preferred_element_type=jnp.float32)
        + biases_float[5]
    )
    output = jnp.roll(
        from_windows(final.reshape(windows, length, width)), (SHIFT, SHIFT), (1, 2)
    ).astype(jnp.bfloat16)
    backing = (
        lax.all_gather(gains, "weight", axis=1, tiled=True),
        lax.all_gather(biases, "weight", axis=1, tiled=True),
        lax.all_gather(qkv_weight, "weight", axis=0, tiled=True),
        lax.all_gather(bias_table, "weight", axis=1, tiled=True),
        lax.all_gather(proj_weight, "weight", axis=0, tiled=True),
        lax.all_gather(fc1_weight, "weight", axis=0, tiled=True),
        lax.all_gather(fc1_bias, "weight", axis=0, tiled=True),
        lax.all_gather(fc2_weight, "weight", axis=0, tiled=True),
    )
    back_gains = backing[0].astype(jnp.float32)
    back_biases = backing[1].astype(jnp.float32)
    back_qkv = backing[2]
    back_table = backing[3].astype(jnp.float32)
    back_proj = backing[4]
    back_expand = backing[5]
    back_reduce = backing[7]
    upstream = to_windows(
        jnp.roll(cotangent, (-SHIFT, -SHIFT), (1, 2)).astype(jnp.float32)
    ).reshape(-1, width)
    upstream_low = upstream.astype(jnp.bfloat16)
    grad_reduce = jnp.einsum(
        "tf,td->fd", activated, upstream_low, preferred_element_type=jnp.float32
    )
    grad_bias_out = jnp.sum(upstream_low.astype(jnp.float32), axis=0)
    grad_act = jnp.einsum(
        "td,fd->tf", upstream_low, back_reduce, preferred_element_type=jnp.float32
    )
    _, gelu_pull = jax.vjp(exact_gelu, hidden)
    grad_hidden = gelu_pull(grad_act)[0].astype(jnp.bfloat16)
    grad_expand = jnp.einsum(
        "td,tf->df", normed_two, grad_hidden, preferred_element_type=jnp.float32
    )
    grad_expand_bias = jnp.sum(grad_hidden.astype(jnp.float32), axis=0)
    grad_normed_two = jnp.einsum(
        "tf,df->td", grad_hidden, back_expand, preferred_element_type=jnp.float32
    )
    _, second_pull = jax.vjp(layer_norm, middle, back_gains[1], back_biases[1])
    grad_mid_norm, grad_gain_two, grad_offset_two = second_pull(grad_normed_two)
    grad_middle = upstream + grad_mid_norm
    middle_low = grad_middle.astype(jnp.bfloat16)
    grad_proj = jnp.einsum("td,te->de", attended, middle_low, preferred_element_type=jnp.float32)
    grad_bias_proj = jnp.sum(middle_low.astype(jnp.float32), axis=0)
    grad_attended = jnp.einsum(
        "te,de->td", middle_low, back_proj, preferred_element_type=jnp.float32
    )
    grad_attended = grad_attended.astype(jnp.bfloat16).reshape(windows, length, heads, size_head)
    back_bias = (
        jnp.dot(table_hot, back_table, precision=highest)
        .reshape(length, length, heads)
        .transpose(2, 0, 1)
    )
    probs = jnp.exp(attention_scores(queries, keys_all, back_bias, mask_tiled, scale) - log_total)
    probs_again = probs.astype(jnp.bfloat16)
    grad_probs = jnp.einsum(
        "wqhe,wkhe->whqk", grad_attended, values_all, preferred_element_type=jnp.float32
    )
    grad_values = jnp.einsum(
        "whqk,wqhe->wkhe", probs_again, grad_attended, preferred_element_type=jnp.float32
    )
    grad_scores = probs * (grad_probs - jnp.sum(probs * grad_probs, axis=-1, keepdims=True))
    scores_low = grad_scores.astype(jnp.bfloat16)
    grad_queries = scale * jnp.einsum(
        "whqk,wkhe->wqhe", scores_low, keys_all, preferred_element_type=jnp.float32
    )
    grad_keys = scale * jnp.einsum(
        "whqk,wqhe->wkhe", scores_low, queries, preferred_element_type=jnp.float32
    )
    grad_rel = (
        jnp.sum(scores_low.astype(jnp.float32), axis=0)
        .transpose(1, 2, 0)
        .reshape(length * length, heads)
    )
    grad_table = jnp.dot(table_hot.T, grad_rel, precision=highest)
    grad_mixed = (
        jnp.stack([grad_queries, grad_keys, grad_values], axis=2)
        .reshape(-1, 3 * width)
        .astype(jnp.bfloat16)
    )
    grad_qkv = jnp.einsum("td,te->de", normed_low, grad_mixed, preferred_element_type=jnp.float32)
    mixed_sums = jnp.sum(grad_mixed.astype(jnp.float32), axis=0).reshape(3, width)
    grad_normed = jnp.einsum("te,de->td", grad_mixed, back_qkv, preferred_element_type=jnp.float32)
    _, first_pull = jax.vjp(layer_norm, flat_in, back_gains[0], back_biases[0])
    grad_in_norm, grad_gain_one, grad_offset_one = first_pull(grad_normed)
    grad_total = (grad_middle + grad_in_norm).reshape(windows, length, width)
    input_grad = jnp.roll(from_windows(grad_total), (SHIFT, SHIFT), (1, 2)).astype(jnp.bfloat16)
    grad_gains = jnp.stack([grad_gain_one, grad_gain_two])
    grad_biases = jnp.stack(
        [
            grad_offset_one,
            grad_offset_two,
            mixed_sums[0],
            mixed_sums[2],
            grad_bias_proj,
            grad_bias_out,
        ]
    )
    owned = (
        lax.psum_scatter(
            grad_gains.astype(jnp.bfloat16), "weight", scatter_dimension=1, tiled=True
        ).astype(jnp.float32),
        lax.psum_scatter(
            grad_biases.astype(jnp.bfloat16), "weight", scatter_dimension=1, tiled=True
        ).astype(jnp.float32),
        lax.psum_scatter(
            grad_qkv.astype(jnp.bfloat16), "weight", scatter_dimension=0, tiled=True
        ).astype(jnp.float32),
        lax.psum_scatter(
            grad_table.astype(jnp.bfloat16), "weight", scatter_dimension=1, tiled=True
        ).astype(jnp.float32),
        lax.psum_scatter(
            grad_proj.astype(jnp.bfloat16), "weight", scatter_dimension=0, tiled=True
        ).astype(jnp.float32),
        lax.psum_scatter(
            grad_expand.astype(jnp.bfloat16), "weight", scatter_dimension=0, tiled=True
        ).astype(jnp.float32),
        lax.psum_scatter(
            grad_expand_bias.astype(jnp.bfloat16), "weight", scatter_dimension=0, tiled=True
        ).astype(jnp.float32),
        lax.psum_scatter(
            grad_reduce.astype(jnp.bfloat16), "weight", scatter_dimension=0, tiled=True
        ).astype(jnp.float32),
    )
    owned = lax.psum(
        (owned[0], owned[1], owned[2], owned[3], owned[4], owned[5], owned[6], owned[7]), "replica"
    )
    return (
        output,
        input_grad,
        owned[0],
        owned[1],
        owned[2],
        owned[3],
        owned[4],
        owned[5],
        owned[6],
        owned[7],
    )


def solution(mesh):
    in_specs = (
        P(("replica", "weight"), None, None, None),
        P(None, "weight"),
        P(None, "weight"),
        P("weight", None),
        P(None, "weight"),
        P("weight", None),
        P("weight", None),
        P("weight"),
        P("weight", None),
        P(),
        P(("replica", "weight"), None, None, None),
    )
    out_specs = (
        P(("replica", "weight"), None, None, None),
        P(("replica", "weight"), None, None, None),
        P(None, "weight"),
        P(None, "weight"),
        P("weight", None),
        P(None, "weight"),
        P("weight", None),
        P("weight", None),
        P("weight"),
        P("weight", None),
    )
    return jax.shard_map(
        per_device, mesh=mesh, in_specs=in_specs, out_specs=out_specs, check_vma=False
    )
```

profile of v0, /device:TPU:0, one launch (start us, length us, event | category | flops | bytes accessed | tf_op | source)
XLA Modules:
  0.0 979.3 jit_solution(10707967917438583953)
XLA Ops:
  62.0 12.4 %all_gather.34 = bf16[512,512]{1,0:T(8,128)(2,1)} all-gather(bf16[128,512]{1,0:T(8,128)(2,1)} %param.16), channel_id=1, replica_groups=mesh['replica'=8,'weight'=4] {'weight'}, dimensions={0}, use_global_device_ids=true | all-gather | bytes 655360 | tf_op jit(solution)/shard_map/all_gather | solution.py:84
  109.9 10.8 %add_convert_fusion.1 = bf16[3136,1536]{1,0:T(8,128)(2,1)} fusion(bf16[512,1536]{1,0:T(8,128)(2,1)} %all-gather.6.cloned.1.call-done, f32[1536]{0:T(1024)S(1)} %pad_maximum_fusion.7, f32[3136,512]{1,0:T(8,128)} %reshape_reshape.15, f32[512]{0:T(512)S(1)} %bitcast.148, f32[512]{0:T(512)S(1)} %bitcast.144, f32[3136]{0:T(1024)S(1)} %rsqrt.25, f32[3136]{0:T(1024)S(1)} %div.43), kind=kOutput, calls=%fused_computation.25 | convolution fusion | flops 4950163456 | bytes 17664512 | tf_op jit(solution)/shard_map/dot_general | solution.py:119
  120.7 41.9 %reshape.257 = bf16[64,49,3,16,32]{4,3,2,1,0:T(8,128)(2,1)} reshape(bf16[3136,1536]{1,0:T(8,128)(2,1)} %add_convert_fusion.1) | data formatting | bytes 19267584 | tf_op jit(solution)/shard_map/reshape | solution.py:122
  162.6 26.9 %fusion.56 = (bf16[64,49,1,16,32]{4,3,2,1,0:T(8,128)(2,1)}, bf16[64,49,1,16,32]{4,3,2,1,0:T(8,128)(2,1)}, bf16[64,49,1,16,32]{4,3,2,1,0:T(8,128)(2,1)}) fusion(bf16[64,49,3,16,32]{4,3,2,1,0:T(8,128)(2,1)} %reshape.257), kind=kLoop, calls=%fused_computation.122 | loop fusion | bytes 19267584 | tf_op jit(solution)/shard_map/slice | solution.py:123
  189.5 17.6 %copy.101 = bf16[64,49,1,16,32]{1,4,3,0,2:T(8,128)(2,1)} copy(bf16[64,49,1,16,32]{4,3,2,1,0:T(8,128)(2,1)} %get-tuple-element.42) | data formatting | bytes 6422528
  207.1 17.6 %copy.100 = bf16[64,49,1,16,32]{1,4,3,0,2:T(8,128)(2,1)} copy(bf16[64,49,1,16,32]{4,3,2,1,0:T(8,128)(2,1)} %get-tuple-element.43) | data formatting | bytes 6422528
  224.8 17.6 %copy.102 = bf16[64,49,1,16,32]{1,4,3,0,2:T(8,128)(2,1)} copy(bf16[64,49,1,16,32]{4,3,2,1,0:T(8,128)(2,1)} %get-tuple-element.44) | data formatting | bytes 6422528
  242.6 19.0 %fusion.60 = (f32[64,16,49]{2,1,0:T(8,128)S(1)}, f32[64,16,49,49]{2,3,1,0:T(8,128)}) fusion(f32[64,49,49]{1,2,0:T(8,128)S(1)} %bitcast.135, f32[16,49,49]{1,2,0:T(8,128)S(1)} %copy.74, bf16[64,49,1,16,32]{1,4,3,0,2:T(8,128)(2,1)} %copy.102, bf16[64,49,1,16,32]{1,4,3,0,2:T(8,128)(2,1)} %copy.101), kind=kOutput, calls=%fused_computation.126 | convolution fusion | flops 167136256 | bytes 17226048 | tf_op jit(solution)/shard_map/wqhe,wkhe->whqk/dot_general | solution.py:60
  261.6 16.3 %exponential_reduce_fusion = f32[64,16,49]{2,1,0:T(8,128)S(1)} fusion(f32[64,16,49,49]{2,3,1,0:T(8,128)} %get-tuple-element.58, f32[64,16,49]{2,1,0:T(8,128)S(1)} %get-tuple-element.57), kind=kLoop, calls=%fused_computation.6 | loop fusion | flops 4867072 | bytes 10235904 | tf_op jit(solution)/shard_map/reduce_sum | solution.py:128
  278.8 17.7 %convert_bitcast_fusion = bf16[64,49,16,32]{1,3,2,0:T(8,128)(2,1)} fusion(bf16[64,49,1,16,32]{1,4,3,0,2:T(8,128)(2,1)} %copy.100, f32[64,16,49,49]{2,3,1,0:T(8,128)} %get-tuple-element.58, f32[64,16,49]{2,1,0:T(8,128)S(1)} %log_add_fusion), kind=kOutput, calls=%fused_computation.41 | convolution fusion | flops 163874816 | bytes 16457728 | tf_op jit(solution)/shard_map/whqk,wkhe->wqhe/dot_general | solution.py:130
  296.5 12.0 %copy.76 = bf16[64,49,16,32]{1,0,3,2:T(8,128)(2,1)} copy(bf16[64,49,16,32]{1,3,2,0:T(8,128)(2,1)} %convert_bitcast_fusion) | data formatting | bytes 6422528 | tf_op jit(solution)/shard_map/convert_element_type | solution.py:133
  308.6 12.0 %convert_element_type.172 = bf16[3136,512]{0,1:T(8,128)(2,1)S(1)} reshape(bf16[64,49,16,32]{1,0,3,2:T(8,128)(2,1)} %copy.76) | data formatting | bytes 6422528 | tf_op jit(solution)/shard_map/convert_element_type | solution.py:133
  331.7 65.2 %multiply_convert_fusion.1 = (bf16[3136,2048]{1,0:T(8,128)(2,1)}, f32[3136,2048]{1,0:T(8,128)}, f32[3136,2048]{1,0:T(8,128)}) fusion(f32[2048]{0:T(1024)S(1)} %bitcast.155, bf16[512,2048]{1,0:T(8,128)(2,1)} %all-gather.8.cloned.1.call-done, f32[3136,512]{1,0:T(8,128)} %copy-done.1, f32[512]{0:T(512)S(1)} %bitcast.159, f32[512]{0:T(512)S(1)} %bitcast.149, ...), kind=kOutput, calls=%fused_computation.10 | convolution fusion | flops 7008583680 | bytes 72782336 | tf_op jit(solution)/shard_map/dot_general | solution.py:138
  396.9 25.9 %fusion.62 = (bf16[2048]{0:T(1024)(128)(2,1)}, bf16[3136,2048]{1,0:T(8,128)(2,1)}) fusion(f32[3136,2048]{1,0:T(8,128)} %get-tuple-element.41, bf16[3136,512]{1,0:T(8,128)(2,1)S(1)} %copy-done.4, bf16[2048,512]{1,0:T(8,128)(2,1)} %all-gather.10.cloned.1.call-done, f32[3136,2048]{1,0:T(8,128)} %get-tuple-element.61, f32[2048]{0:T(1024)S(1)} %bitcast.156), kind=kOutput, calls=%fused_computation.128 | convolution fusion | flops 6679427072 | bytes 69545984 | tf_op jit(solution)/shard_map/td,fd->tf/dot_general | solution.py:175
  422.8 18.1 %multiply_reduce_fusion.2 = (bf16[512]{0:T(512)(128)(2,1)S(1)}, f32[3136]{0:T(1024)S(1)}, bf16[512]{0:T(512)(128)(2,1)}, f32[3136,512]{1,0:T(8,128)S(1)}) fusion(f32[3136,512]{1,0:T(8,128)} %copy-done.1, f32[3136]{0:T(1024)S(1)} %fusion.43, f32[3136]{0:T(1024)S(1)} %broadcast_multiply_fusion.1, f32[512]{0:T(512)S(1)} %bitcast.150, ...), kind=kOutput, calls=%fused_computation.48 | convolution fusion | flops 6589509632 | bytes 27828992 | tf_op jit(solution)/shard_map/tf,df->td/dot_general | solution.py:184
  452.7 10.8 %reshape.258 = bf16[64,49,16,32]{3,2,1,0:T(8,128)(2,1)} reshape(bf16[3136,512]{1,0:T(8,128)(2,1)S(1)} %convolution_convert_fusion) | data formatting | bytes 6422528 | tf_op jit(solution)/shard_map/reshape | solution.py:196
  463.5 17.7 %copy.80 = bf16[64,49,16,32]{1,3,2,0:T(8,128)(2,1)} copy(bf16[64,49,16,32]{3,2,1,0:T(8,128)(2,1)} %reshape.258) | data formatting | bytes 6422528 | tf_op jit(solution)/shard_map/reshape | solution.py:196
  481.1 18.4 %convolution_bitcast_fusion = bf16[64,49,1,16,32]{1,4,3,0,2:T(8,128)(2,1)} fusion(bf16[64,49,16,32]{1,3,2,0:T(8,128)(2,1)} %copy.80, f32[64,16,49,49]{2,3,1,0:T(8,128)} %get-tuple-element.58, f32[64,16,49]{2,1,0:T(8,128)S(1)} %copy-done.11), kind=kOutput, calls=%fused_computation.30 | convolution fusion | flops 162269184 | bytes 16457728 | tf_op jit(solution)/shard_map/whqk,wqhe->wkhe/dot_general | solution.py:207
  499.5 25.5 %multiply_reduce_fusion = (f32[64,16,49]{2,1,0:T(8,128)S(1)}, f32[64,16,49,49]{2,3,1,0:T(8,128)}) fusion(f32[64,16,49,49]{2,3,1,0:T(8,128)} %get-tuple-element.58, f32[64,16,49]{2,1,0:T(8,128)S(1)} %copy-done.11, bf16[64,49,16,32]{1,3,2,0:T(8,128)(2,1)} %copy.80, bf16[64,49,1,16,32]{1,4,3,0,2:T(8,128)(2,1)} %copy.100), kind=kOutput, calls=%fused_computation.4 | convolution fusion | flops 164677632 | bytes 26492928 | tf_op jit(solution)/shard_map/wqhe,wkhe->whqk/dot_general | solution.py:204
  525.0 27.6 %convert_reduce_fusion = (f32[16,49,49]{1,2,0:T(8,128)}, bf16[64,16,49,49]{2,3,1,0:T(8,128)(2,1)}) fusion(f32[64,16,49,49]{2,3,1,0:T(8,128)} %get-tuple-element.64, f32[64,16,49]{2,1,0:T(8,128)S(1)} %get-tuple-element.63, f32[64,16,49,49]{2,3,1,0:T(8,128)} %get-tuple-element.58, f32[64,16,49]{2,1,0:T(8,128)S(1)} %copy-done.11), kind=kLoop, calls=%fused_computation.2 | loop fusion | flops 14713328 | bytes 25141312 | tf_op jit(solution)/shard_map/reduce_sum | solution.py:219
  552.6 14.3 %multiply_bitcast_fusion = bf16[64,49,1,16,32]{1,4,3,0,2:T(8,128)(2,1)} fusion(bf16[64,16,49,49]{2,3,1,0:T(8,128)(2,1)} %get-tuple-element.27, bf16[64,49,1,16,32]{1,4,3,0,2:T(8,128)(2,1)} %copy.101), kind=kOutput, calls=%fused_computation.26 | convolution fusion | flops 160563200 | bytes 11339776 | tf_op jit(solution)/shard_map/whqk,wqhe->wkhe/dot_general | solution.py:215
  567.0 11.8 %multiply_bitcast_fusion.1 = bf16[64,49,1,16,32]{1,4,3,0,2:T(8,128)(2,1)} fusion(bf16[64,16,49,49]{2,3,1,0:T(8,128)(2,1)} %get-tuple-element.27, bf16[64,49,1,16,32]{1,4,3,0,2:T(8,128)(2,1)} %copy.102), kind=kOutput, calls=%fused_computation.27 | convolution fusion | flops 160563200 | bytes 11339776 | tf_op jit(solution)/shard_map/whqk,wkhe->wqhe/dot_general | solution.py:212
  578.8 17.7 %fusion.52 = (bf16[3,16,32]{2,1,0:T(8,128)(2,1)S(1)}, bf16[64,49,3,16,32]{1,4,3,0,2:T(8,128)(2,1)}) fusion(bf16[64,49,1,16,32]{1,4,3,0,2:T(8,128)(2,1)} %convolution_bitcast_fusion, bf16[64,49,1,16,32]{1,4,3,0,2:T(8,128)(2,1)} %multiply_bitcast_fusion, bf16[64,49,1,16,32]{1,4,3,0,2:T(8,128)(2,1)} %multiply_bitcast_fusion.1), kind=kLoop, calls=%fused_computation.119 | loop fusion | flops 14449152 | bytes 19270656 | tf_op jit(solution)/shard_map/reduce_sum | solution.py:230
  596.5 26.8 %copy.85 = bf16[64,49,3,16,32]{1,0,4,3,2:T(8,128)(2,1)} copy(bf16[64,49,3,16,32]{1,4,3,0,2:T(8,128)(2,1)} %get-tuple-element.35) | data formatting | bytes 19267584 | tf_op jit(solution)/shard_map/convert_element_type | solution.py:227
  623.3 37.6 %convert_element_type.182 = bf16[3136,1536]{0,1:T(8,128)(2,1)} reshape(bf16[64,49,3,16,32]{1,0,4,3,2:T(8,128)(2,1)} %copy.85) | data formatting | bytes 19267584 | tf_op jit(solution)/shard_map/convert_element_type | solution.py:227
  661.0 14.8 %multiply_reduce_fusion.3 = (bf16[512]{0:T(512)(128)(2,1)S(1)}, f32[3136]{0:T(1024)S(1)}, bf16[512]{0:T(512)(128)(2,1)S(1)}, f32[3136,512]{1,0:T(8,128)}) fusion(f32[3136,512]{1,0:T(8,128)} %reshape_reshape.15, f32[3136]{0:T(1024)S(1)} %copy-done.29, f32[3136]{0:T(1024)S(1)} %copy-done.27, f32[512]{0:T(512)S(1)} %bitcast.145, ...), kind=kOutput, calls=%fused_computation.49 | convolution fusion | flops 4945342464 | bytes 24093440 | tf_op jit(solution)/shard_map/te,de->td/dot_general | solution.py:231
  693.0 11.2 %convolution_convert_fusion.2 = bf16[2048,512]{1,0:T(8,128)(2,1)} fusion(bf16[3136,2048]{1,0:T(8,128)(2,1)} %get-tuple-element.40, bf16[3136,512]{1,0:T(8,128)(2,1)S(1)} %copy-done.5), kind=kOutput, calls=%fused_computation.79 | convolution fusion | flops 6577717248 | bytes 18153472 | tf_op jit(solution)/shard_map/tf,td->fd/dot_general | solution.py:171
  706.4 13.4 %convolution_convert_fusion.1 = bf16[512,2048]{1,0:T(8,128)(2,1)} fusion(bf16[3136,2048]{1,0:T(8,128)(2,1)} %get-tuple-element.67, f32[3136,512]{1,0:T(8,128)} %copy-done.1, f32[512]{0:T(512)S(1)} %bitcast.160, f32[512]{0:T(512)S(1)} %bitcast.152, f32[3136]{0:T(1024)S(1)} %copy-done.31, f32[3136]{0:T(1024)S(1)} %copy-done.21), kind=kOutput, calls=%fused_computation.78 | convolution fusion | flops 6585745408 | bytes 21393920 | tf_op jit(solution)/shard_map/td,tf->df/dot_general | solution.py:180
  719.9 12.6 %fusion.23 = bf16[3136,512]{1,0:T(8,128)(2,1)} fusion(f32[3136,512]{1,0:T(8,128)} %copy-done.1, bf16[3136,2048]{1,0:T(8,128)(2,1)} %get-tuple-element.40, bf16[2048,512]{1,0:T(8,128)(2,1)} %all-gather.10.cloned.1.call-done, f32[512]{0:T(512)S(1)} %bitcast.158), kind=kOutput, calls=%fused_computation.47 | convolution fusion | flops 6581485568 | bytes 24578048 | tf_op jit(solution)/shard_map/dot_general | solution.py:144
  791.3 16.9 %reduce-scatter.17.cloned.1.call-done = bf16[512,512]{1,0:T(8,128)(2,1)} async-done(((bf16[2048,512]{1,0:T(8,128)(2,1)}), bf16[512,512]{1,0:T(8,128)(2,1)}) %reduce-scatter.17.cloned.1.call-update) | async-done | bytes 524304 | tf_op jit(solution)/shard_map/reduce_scatter | solution.py:269
  808.1 34.2 %reduce-scatter.15.cloned.1.call-done = bf16[128,2048]{1,0:T(8,128)(2,1)} async-done(((bf16[512,2048]{1,0:T(8,128)(2,1)}), bf16[128,2048]{1,0:T(8,128)(2,1)}) %reduce-scatter.15.cloned.1.call-update) | async-done | bytes 524304 | tf_op jit(solution)/shard_map/reduce_scatter | solution.py:263
  842.3 130.0 %all-reduce.5 = (f32[2,128]{1,0:T(2,128)}, f32[6,128]{1,0:T(8,128)}, f32[128,1536]{1,0:T(8,128)}, f32[169,4]{0,1:T(4,128)}, f32[128,512]{1,0:T(8,128)}, /*index=...) all-reduce(bf16[2,128]{1,0:T(2,128)(2,1)S(1)} %copy.93, ...), channel_id=1, replica_groups=mesh['replica'=8,'weight'=4] {'replica'}, use_global_device_ids=true, to_apply=%region_14.15 | all-reduce | flops 788644 | bytes 4734240 | tf_op jit(solution)/shard_map/psum | solution.py:273
  (233 shorter events, 190.4 us)
Async XLA Ops:
  7.2 102.7 %all-gather.6.cloned.1.call-start = ((), (), s32[]{:S(2)}) async-start(), calls=%async_computation.6 | async-start | bytes 1966080 | tf_op jit(solution)/shard_map/all_gather | solution.py:82
  7.9 323.7 %all-gather.8.cloned.1.call-start = ((), (), s32[]{:S(2)}) async-start(), calls=%async_computation.7 | async-start | bytes 2621440 | tf_op jit(solution)/shard_map/all_gather | solution.py:85
  8.7 388.2 %all-gather.10.cloned.1.call-start = ((), (), s32[]{:S(2)}) async-start(), calls=%async_computation.8 | async-start | bytes 2621440 | tf_op jit(solution)/shard_map/all_gather | solution.py:87
  9.4 780.2 %reduce-scatter.19.cloned.1.call-start = ((), (), s32[]{:S(2)}) async-start(), calls=%async_computation.13 | async-start | bytes 163840
  24.1 85.8 %copy-start.26 = (f32[3136]{0:T(1024)}, f32[3136]{0:T(1024)S(1)}, u32[]{:S(2)}) copy-start(f32[3136]{0:T(1024)S(1)} %div.43) | copy-start | bytes 37636
  24.1 20.0 %copy-start.47 = (bf16[512]{0:T(512)(128)(2,1)S(1)}, bf16[512]{0:T(512)(128)(2,1)}, u32[]{:S(2)}) copy-start(bf16[512]{0:T(512)(128)(2,1)} %param.18) | copy-start | bytes 3076
  24.1 25.5 %copy-start.42 = (bf16[6,128]{1,0:T(8,128)(2,1)S(1)}, bf16[6,128]{1,0:T(8,128)(2,1)}, u32[]{:S(2)}) copy-start(bf16[6,128]{1,0:T(8,128)(2,1)} %param.13) | copy-start | bytes 4612
  24.2 31.2 %copy-start.43 = (bf16[169,4]{0,1:T(4,128)(2,1)S(1)}, bf16[169,4]{0,1:T(4,128)(2,1)}, u32[]{:S(2)}) copy-start(bf16[169,4]{0,1:T(4,128)(2,1)} %param.15) | copy-start | bytes 4060
  24.2 36.4 %copy-start.32 = (s32[49,49]{1,0:T(8,128)S(1)}, s32[49,49]{1,0:T(8,128)}, u32[]{:S(2)}) copy-start(s32[49,49]{1,0:T(8,128)} %param.20) | copy-start | bytes 28816
  44.1 65.8 %copy-start.33 = (f32[1,512]{1,0:T(1,128)}, f32[1,512]{1,0:T(1,128)S(1)}, u32[]{:S(2)}) copy-start(f32[1,512]{1,0:T(1,128)S(1)} %get-tuple-element.56) | copy-start | bytes 6148
  44.1 396.7 %copy-start.37 = (f32[1,512]{1,0:T(1,128)}, f32[1,512]{1,0:T(1,128)S(1)}, u32[]{:S(2)}) copy-start(f32[1,512]{1,0:T(1,128)S(1)} %get-tuple-element.55) | copy-start | bytes 6148
  55.4 276.2 %copy-start.45 = (f32[1,512]{1,0:T(1,128)}, f32[1,512]{1,0:T(1,128)S(1)}, u32[]{:S(2)}) copy-start(f32[1,512]{1,0:T(1,128)S(1)} %get-tuple-element.50) | copy-start | bytes 6148
  102.0 18.7 %copy-start.24 = (f32[3136]{0:T(1024)}, f32[3136]{0:T(1024)S(1)}, u32[]{:S(2)}) copy-start(f32[3136]{0:T(1024)S(1)} %add.198) | copy-start | bytes 37636
  102.1 18.7 %copy-start.28 = (f32[3136]{0:T(1024)}, f32[3136]{0:T(1024)S(1)}, u32[]{:S(2)}) copy-start(f32[3136]{0:T(1024)S(1)} %rsqrt.25) | copy-start | bytes 37636
  326.9 113.9 %copy-start.20 = (f32[3136]{0:T(1024)}, f32[3136]{0:T(1024)S(1)}, u32[]{:S(2)}) copy-start(f32[3136]{0:T(1024)S(1)} %broadcast_multiply_fusion.1) | copy-start | bytes 37636
  331.6 109.3 %copy-start.30 = (f32[3136]{0:T(1024)}, f32[3136]{0:T(1024)S(1)}, u32[]{:S(2)}) copy-start(f32[3136]{0:T(1024)S(1)} %fusion.43) | copy-start | bytes 37636
  331.6 65.2 %copy-start.4 = (bf16[3136,512]{1,0:T(8,128)(2,1)S(1)}, bf16[3136,512]{1,0:T(8,128)(2,1)}, u32[]{:S(2)}) copy-start(bf16[3136,512]{1,0:T(8,128)(2,1)} %reshape_reshape.17) | copy-start | bytes 9633796
  422.8 18.1 %copy-start.23 = (f32[3136]{0:T(1024)S(1)}, f32[3136]{0:T(1024)}, u32[]{:S(2)}) copy-start(f32[3136]{0:T(1024)} %copy-done.22) | copy-start | bytes 37636
  422.8 18.1 %copy-start.2 = (f32[3136,512]{1,0:T(8,128)S(1)}, f32[3136,512]{1,0:T(8,128)}, u32[]{:S(2)}) copy-start(f32[3136,512]{1,0:T(8,128)} %copy-done.1) | copy-start | bytes 19267588
  463.4 17.7 %copy-start.11 = (f32[64,16,49]{2,1,0:T(8,128)S(1)}, f32[64,16,49]{2,1,0:T(8,128)}, u32[]{:S(2)}) copy-start(f32[64,16,49]{2,1,0:T(8,128)} %copy-done.10) | copy-start | bytes 602116
  623.3 37.6 %copy-start.27 = (f32[3136]{0:T(1024)S(1)}, f32[3136]{0:T(1024)}, u32[]{:S(2)}) copy-start(f32[3136]{0:T(1024)} %copy-done.26) | copy-start | bytes 37636
  623.3 37.6 %copy-start.29 = (f32[3136]{0:T(1024)S(1)}, f32[3136]{0:T(1024)}, u32[]{:S(2)}) copy-start(f32[3136]{0:T(1024)} %copy-done.28) | copy-start | bytes 37636
  623.3 37.6 %copy-start.34 = (f32[1,512]{1,0:T(1,128)S(1)}, f32[1,512]{1,0:T(1,128)}, u32[]{:S(2)}) copy-start(f32[1,512]{1,0:T(1,128)} %copy-done.33) | copy-start | bytes 6148
  661.0 16.0 %copy-start.39 = (bf16[1,512]{1,0:T(2,128)(2,1)S(1)}, bf16[1,512]{1,0:T(2,128)(2,1)}, u32[]{:S(2)}) copy-start(bf16[1,512]{1,0:T(2,128)(2,1)} %stack.42) | copy-start | bytes 3076
  661.0 16.9 %copy-start.9 = (bf16[3136,512]{0,1:T(8,128)(2,1)S(1)}, bf16[3136,512]{0,1:T(8,128)(2,1)}, u32[]{:S(2)}) copy-start(bf16[3136,512]{0,1:T(8,128)(2,1)} %copy-done.8) | copy-start | bytes 9633796
  676.6 113.8 %reduce-scatter.21.cloned.1.call-start = ((), (), s32[]{:S(2)}) async-start(), calls=%async_computation.14 | async-start | bytes 163840
  677.8 113.5 %reduce-scatter.13.cloned.1.call-start = ((), (), s32[]{:S(2)}) async-start(), calls=%async_computation.10 | async-start | bytes 655360 | tf_op jit(solution)/shard_map/reduce_scatter | solution.py:260
  682.5 108.8 %reduce-scatter.11.cloned.1.call-start = ((), (), s32[]{:S(2)}) async-start(), calls=%async_computation.9 | async-start | bytes 1966080 | tf_op jit(solution)/shard_map/reduce_scatter | solution.py:254
  692.8 115.3 %reduce-scatter.17.cloned.1.call-start = ((), (), s32[]{:S(2)}) async-start(), calls=%async_computation.12 | async-start | bytes 2621440 | tf_op jit(solution)/shard_map/reduce_scatter | solution.py:269
  704.2 138.1 %reduce-scatter.15.cloned.1.call-start = ((), (), s32[]{:S(2)}) async-start(), calls=%async_computation.11 | async-start | bytes 2621440 | tf_op jit(solution)/shard_map/reduce_scatter | solution.py:263
  761.4 21.6 %copy-start.6 = (bf16[16,11,14,512]{3,0,2,1:T(8,128)(2,1)S(1)}, bf16[16,11,14,512]{3,0,2,1:T(8,128)(2,1)}, u32[]{:S(2)}) copy-start(bf16[16,11,14,512]{3,0,2,1:T(8,128)(2,1)} %slice.156) | copy-start | bytes 7569412
  761.4 21.6 %copy-start.12 = (bf16[16,3,14,512]{3,0,2,1:T(8,128)(2,1)S(1)}, bf16[16,3,14,512]{3,0,2,1:T(8,128)(2,1)}, u32[]{:S(2)}) copy-start(bf16[16,3,14,512]{3,0,2,1:T(8,128)(2,1)} %slice.155) | copy-start | bytes 2064388
  (32 other events, 261.4 us)
Sparse Core Ops, SparseCore 0:
  9.6 22.3 all-gather.5
  33.5 22.6 all-gather.7
  57.8 25.2 all-gather.9
  676.8 19.7 reduce-scatter.18
  699.0 19.6 reduce-scatter.20
  721.5 21.6 reduce-scatter.12
  745.9 28.1 reduce-scatter.10
  776.7 31.4 reduce-scatter.16
  810.8 31.4 reduce-scatter.14
where the time goes:
time: 995 us; the launch traced here: 979 us
  local copies, waits for them, and re-layouts  319 us (32%)
  matrix products  303 us (30%)
  blocking collectives  174 us (17%)
  other arithmetic  113 us (11%)
  waiting for transfers between devices  53.2 us (5%)
  between operations  16.5 us (2%)
    psum x1, blocking collectives, per_device(): lax.psum((owned[0], owned[1], owned[2], owned[3], owned[4], owned[5], own...  130 us
    unnamed x120, local copies, waits for them, and re-layouts  68.8 us
    dot_general x1, matrix products, per_device(): jnp.dot(normed_two, full_expand, preferred_element_type=jnp.float32)  65.2 us
    convert_element_type x2, local copies, waits for them, and re-layouts, per_device(): grad_mixed = jnp.stack([grad_queries, grad_keys, grad_values], axis=2).re...  64.4 us
    reshape x1, local copies, waits for them, and re-layouts, per_device(): mixed = mixed.reshape(windows, length, 3, heads, size_head)  41.9 us
    reduce_scatter x1, waiting for transfers between devices, per_device(): lax.psum_scatter(grad_expand.astype(jnp.bfloat16), 'weight', scatter_dime...  34.2 us
    reshape x2, local copies, waits for them, and re-layouts, per_device(): grad_attended.astype(jnp.bfloat16)  28.4 us
    reduce_sum x1, other arithmetic, per_device(): jnp.sum(scores_low.astype(jnp.float32), axis=0).transpose(1, 2, 0)  27.6 us
  transfers between devices with their start and end apart: 9, of which 2 were waited for; matrix products, arithmetic and copies ran while one was open for 46% of the time, Pallas kernels for 0%

commit v1 on v0

v1 whole, which is shorter than its diff:
```python
import functools

import jax
import jax.numpy as jnp
import numpy as np
from jax import lax
from jax.experimental import pallas as pl
from jax.experimental.pallas import tpu as pltpu
from jax.sharding import PartitionSpec as P

GRID = 14
WIN = 7
SHIFT = 3
ACROSS = GRID // WIN
LEN = WIN * WIN
SLOT = 56
ROWS = ACROSS * ACROSS * SLOT
LINE = 16
SPAN = (2 * WIN - 1) ** 2
GROUP = 4
BATCH = 2
F32 = jnp.float32
BF16 = jnp.bfloat16
EPSILON = 1e-05


def token_permutation():
    matrix = np.zeros((ROWS, GRID * LINE), np.float32)
    for w in range(ACROSS * ACROSS):
        for i in range(LEN):
            row = ((w // ACROSS) * WIN + i // WIN + SHIFT) % GRID
            col = ((w % ACROSS) * WIN + i % WIN + SHIFT) % GRID
            matrix[w * SLOT + i, row * LINE + col] = 1.0
    return matrix


def region_mask():
    places = np.arange(GRID)
    bands = (places >= GRID - WIN).astype(np.int32) + (places >= GRID - SHIFT).astype(np.int32)
    labels = bands[:, None] * 3 + bands[None, :]
    labels = (
        labels.reshape(ACROSS, WIN, ACROSS, WIN)
        .transpose(0, 2, 1, 3)
        .reshape(ACROSS * ACROSS, LEN)
    )
    mask = np.zeros((ACROSS * ACROSS, SLOT, SLOT), np.float32)
    mask[:, :LEN, :LEN] = np.where(labels[:, :, None] == labels[:, None, :], 0.0, -100.0)
    mask[:, LEN:, :] = -1e30
    return mask


def dot(a, b):
    return jnp.dot(a, b, preferred_element_type=F32)


def dot_t(a, b):
    return lax.dot_general(a, b, (((1,), (1,)), ((), ())), preferred_element_type=F32)


def t_dot(a, b):
    return lax.dot_general(a, b, (((0,), (0,)), ((), ())), preferred_element_type=F32)


def normalise(values):
    center = values - jnp.mean(values, axis=-1, keepdims=True)
    spread = jnp.mean(center * center, axis=-1, keepdims=True)
    inverse = lax.rsqrt(spread + EPSILON)
    return center * inverse, inverse


def norm_back(grad, unit, inverse, gain):
    scaled = grad * gain
    return inverse * (
        scaled
        - jnp.mean(scaled, axis=-1, keepdims=True)
        - unit * jnp.mean(scaled * unit, axis=-1, keepdims=True)
    )


def column_sum(values):
    return jnp.sum(values, axis=0, keepdims=True)


def gelu_parts(hidden):
    bell = jnp.exp(hidden * hidden * -0.5)
    step = 1.0 / (1.0 + (0.3275911 * 0.7071067811865476) * jnp.abs(hidden))
    series = step * (
        0.5 * 0.254829592
        + step
        * (
            0.5 * -0.284496736
            + step * (0.5 * 1.421413741 + step * (0.5 * -1.453152027 + step * (0.5 * 1.061405429)))
        )
    )
    tail = series * bell
    below = jnp.where(hidden < 0.0, tail, 1.0 - tail)
    return below, bell * 0.3989422804014327


def head_masks(width_head):
    lanes = lax.broadcasted_iota(jnp.int32, (SLOT, GROUP * width_head), 1)
    return [
        (lanes >= h * width_head) & (lanes < (h + 1) * width_head) for h in range(GROUP)
    ]


def expand(block, masks):
    return jnp.concatenate([jnp.where(m, block, 0.0) for m in masks], axis=0).astype(BF16)


def collect(rows, masks):
    total = jnp.where(masks[0], rows[:SLOT], 0.0)
    for h in range(1, GROUP):
        total = jnp.where(masks[h], rows[h * SLOT : (h + 1) * SLOT], total)
    return total


def read_image(ref, at, grid_ref, perm_ref):
    for r in range(GRID):
        grid_ref[r * LINE : r * LINE + GRID, :] = ref[at, r]
    return dot(perm_ref[...], grid_ref[...])


def write_image(ref, at, values, back_ref):
    lines = dot(back_ref[...], values).astype(BF16)
    for r in range(GRID):
        ref[at, r] = lines[r * LINE : r * LINE + GRID]


def forward_kernel(
    width_head,
    images, cotangent, weights, reduce, vectors, qkv_bias, expand_bias, rel_bias, mask, perm, back,
    output, mixed_out, attended_out, middle_out, probs_out, expand_grad, reduce_grad, sums, expand_sums,
    grid_rows, inputs, ups, mixed, attended, expand_acc, reduce_acc,
):
    width = inputs.shape[1]
    hidden_width = expand_bias.shape[1]
    step = pl.program_id(0)

    @pl.when(step == 0)
    def _():
        grid_rows[...] = jnp.zeros_like(grid_rows)
        expand_acc[...] = jnp.zeros_like(expand_acc)
        reduce_acc[...] = jnp.zeros_like(reduce_acc)
        sums[...] = jnp.zeros_like(sums)
        expand_sums[...] = jnp.zeros_like(expand_sums)

    for b in range(BATCH):
        inputs[b * ROWS : (b + 1) * ROWS, :] = read_image(images, b, grid_rows, perm)
        ups[b * ROWS : (b + 1) * ROWS, :] = read_image(cotangent, b, grid_rows, perm)
    unit, _ = normalise(inputs[...])
    normed = (unit * vectors[0:1, :] + vectors[2:3, :]).astype(BF16)
    mixed_low = (dot(normed, weights[:, : 3 * width]) + qkv_bias[...]).astype(BF16)
    mixed_out[...] = mixed_low
    mixed[...] = mixed_low.astype(F32)
    scale = width_head ** (-0.5)

    def attend(w, carry):
        masks = head_masks(width_head)
        rows = pl.ds(pl.multiple_of(w * SLOT, 8), SLOT)
        region = mask[lax.rem(w, ACROSS * ACROSS)]
        size = GROUP * width_head
        for g in range(width // size):
            queries = mixed[rows, g * size : (g + 1) * size].astype(BF16)
            keys = expand(mixed[rows, width + g * size : width + (g + 1) * size], masks)
            values = expand(mixed[rows, 2 * width + g * size : 2 * width + (g + 1) * size], masks)
            scores = dot_t(keys, queries) * scale + rel_bias[g]
            scores = scores.reshape(GROUP, SLOT, SLOT) + region[None]
            raised = jnp.exp(scores - jnp.max(scores, axis=1, keepdims=True))
            probs = raised * (1.0 / jnp.sum(raised, axis=1, keepdims=True))
            probs = probs.reshape(GROUP * SLOT, SLOT).astype(BF16)
            probs_out[w * (width // size) + g] = probs
            attended[rows, g * size : (g + 1) * size] = t_dot(probs, values)
        return carry

    lax.fori_loop(0, BATCH * ACROSS * ACROSS, attend, 0)

    attended_low = attended[...].astype(BF16)
    attended_out[...] = attended_low
    middle = inputs[...] + dot(attended_low, weights[:, 3 * width : 4 * width]) + vectors[6:7, :]
    unit, inverse = normalise(middle)
    normed_two = (unit * vectors[1:2, :] + vectors[3:4, :]).astype(BF16)
    up = ups[...]
    up_low = up.astype(BF16)
    final = middle + vectors[7:8, :]
    grad_normed = jnp.zeros_like(final)
    chunk = 512
    for c in range(hidden_width // chunk):
        part = slice(c * chunk, (c + 1) * chunk)
        expand_part = weights[:, 4 * width + c * chunk : 4 * width + (c + 1) * chunk]
        hidden = dot(normed_two, expand_part) + expand_bias[:, part]
        below, density = gelu_parts(hidden)
        activated = (hidden * below).astype(BF16)
        final = final + dot(activated, reduce[part, :])
        grad_act = dot_t(up_low, reduce[part, :])
        grad_hidden = (grad_act * (below + hidden * density)).astype(BF16)
        expand_sums[:, part] += column_sum(grad_hidden.astype(F32))
        expand_acc[:, part] += t_dot(normed_two, grad_hidden)
        reduce_acc[part, :] += t_dot(activated, up_low)
        grad_normed = grad_normed + dot_t(grad_hidden, expand_part)
    sums[0:1, :] += column_sum(grad_normed * unit)
    sums[1:2, :] += column_sum(grad_normed)
    sums[2:3, :] += column_sum(up)
    middle_out[...] = up + norm_back(grad_normed, unit, inverse, vectors[1:2, :])
    final_low = final.astype(BF16)
    for b in range(BATCH):
        write_image(output, b, final_low[b * ROWS : (b + 1) * ROWS], back)

    @pl.when(step == pl.num_programs(0) - 1)
    def _():
        expand_grad[...] = expand_acc[...].astype(BF16)
        reduce_grad[...] = reduce_acc[...].astype(BF16)


def backward_kernel(
    width_head,
    images, weights, vectors, mixed_in, attended_in, middle_in, probs_in, perm, back,
    input_grad, weight_grad, sums, mixed_sums, rel_grad,
    grid_rows, inputs, mixed, grad_attended, grad_mixed, weight_acc,
):
    width = inputs.shape[1]
    step = pl.program_id(0)

    @pl.when(step == 0)
    def _():
        grid_rows[...] = jnp.zeros_like(grid_rows)
        weight_acc[...] = jnp.zeros_like(weight_acc)
        sums[...] = jnp.zeros_like(sums)
        mixed_sums[...] = jnp.zeros_like(mixed_sums)
        rel_grad[...] = jnp.zeros_like(rel_grad)

    for b in range(BATCH):
        inputs[b * ROWS : (b + 1) * ROWS, :] = read_image(images, b, grid_rows, perm)
    mixed[...] = mixed_in[...].astype(F32)
    middle_low = middle_in[...].astype(BF16)
    weight_acc[:, 3 * width :] += t_dot(attended_in[...], middle_low)
    sums[0:1, :] += column_sum(middle_low.astype(F32))
    grad_attended[...] = dot_t(middle_low, weights[:, 3 * width :]).astype(BF16).astype(F32)
    scale = width_head ** (-0.5)

    def attend(w, carry):
        masks = head_masks(width_head)
        rows = pl.ds(pl.multiple_of(w * SLOT, 8), SLOT)
        size = GROUP * width_head
        for g in range(width // size):
            here = slice(g * size, (g + 1) * size)
            queries = mixed[rows, here].astype(BF16)
            keys = expand(mixed[rows, width + g * size : width + (g + 1) * size], masks)
            values = expand(mixed[rows, 2 * width + g * size : 2 * width + (g + 1) * size], masks)
            grad = grad_attended[rows, here].astype(BF16)
            probs_low = probs_in[w * (width // size) + g]
            probs = probs_low.astype(F32).reshape(GROUP, SLOT, SLOT)
            grad_probs = dot_t(values, grad).reshape(GROUP, SLOT, SLOT)
            grad_values = collect(dot(probs_low, grad), masks)
            shift = jnp.sum(probs * grad_probs, axis=1, keepdims=True)
            grad_scores = (probs * (grad_probs - shift)).reshape(GROUP * SLOT, SLOT).astype(BF16)
            rel_grad[g] += grad_scores.astype(F32)
            grad_mixed[rows, here] = scale * t_dot(grad_scores, keys)
            grad_mixed[rows, width + g * size : width + (g + 1) * size] = scale * collect(
                dot(grad_scores, queries), masks
            )
            grad_mixed[rows, 2 * width + g * size : 2 * width + (g + 1) * size] = grad_values
        return carry

    lax.fori_loop(0, BATCH * ACROSS * ACROSS, attend, 0)

    grad_low = grad_mixed[...].astype(BF16)
    mixed_sums[...] += column_sum(grad_low.astype(F32))
    unit, inverse = normalise(inputs[...])
    normed = (unit * vectors[0:1, :] + vectors[2:3, :]).astype(BF16)
    weight_acc[:, : 3 * width] += t_dot(normed, grad_low)
    grad_normed = dot_t(grad_low, weights[:, : 3 * width])
    sums[1:2, :] += column_sum(grad_normed * unit)
    sums[2:3, :] += column_sum(grad_normed)
    total = middle_in[...] + norm_back(grad_normed, unit, inverse, vectors[0:1, :])
    total_low = total.astype(BF16)
    for b in range(BATCH):
        write_image(input_grad, b, total_low[b * ROWS : (b + 1) * ROWS], back)

    @pl.when(step == pl.num_programs(0) - 1)
    def _():
        weight_grad[...] = weight_acc[...].astype(BF16)


def whole(shape):
    return pl.BlockSpec(shape, lambda i: (0,) * len(shape), pipeline_mode=pl.Buffered(1))


def kept(shape):
    return pl.BlockSpec(shape, lambda i: (0,) * len(shape))


def per_step(*shape):
    return pl.BlockSpec(shape, lambda i: (i,) + (0,) * (len(shape) - 1))


def reduce_owned(grad):
    mine = lax.psum_scatter(grad, "weight", scatter_dimension=0, tiled=True)
    return lax.psum(mine, "replica")


def per_device(
    shards, images, gains, biases, qkv_weight, bias_table, proj_weight, fc1_weight, fc1_bias,
    fc2_weight, rel_index, cotangent,
):
    number, width = images.shape[0], images.shape[-1]
    heads = bias_table.shape[1] * shards
    width_head = width // heads
    hidden_width = fc1_weight.shape[1]
    own = width // shards
    groups = heads // GROUP
    steps = number // BATCH
    rows = BATCH * ROWS
    windows = BATCH * ACROSS * ACROSS

    weights = lax.all_gather(
        jnp.concatenate([qkv_weight, proj_weight, fc1_weight], axis=1), "weight", axis=0, tiled=True
    )
    reduce = lax.all_gather(fc2_weight, "weight", axis=0, tiled=True)
    hidden_lines = hidden_width // shards // own
    table_own = bias_table.T.reshape(-1)
    table_lines = -(-table_own.shape[0] // own)
    table_pad = jnp.pad(table_own, (0, table_lines * own - table_own.shape[0]))
    small = jnp.concatenate(
        [gains, biases, fc1_bias.reshape(hidden_lines, own), table_pad.reshape(table_lines, own)]
    )
    small = lax.all_gather(small, "weight", axis=0)
    vectors = small[:, :8].transpose(1, 0, 2).reshape(8, width).astype(F32)
    expand_bias = small[:, 8 : 8 + hidden_lines].reshape(1, hidden_width).astype(F32)
    table = small[:, 8 + hidden_lines :].reshape(shards, -1)[:, : table_own.shape[0]]
    table = table.reshape(heads, SPAN)
    qkv_bias = jnp.concatenate([vectors[4], jnp.zeros_like(vectors[4]), vectors[5]])[None]

    entries = jnp.arange(SPAN, dtype=jnp.int32)
    hot = (rel_index.T.reshape(-1)[None, :] == entries[:, None]).astype(BF16)
    rel_bias = dot(table, hot).reshape(heads, LEN, LEN)
    rel_bias = jnp.pad(rel_bias, ((0, 0), (0, SLOT - LEN), (0, SLOT - LEN)))
    rel_bias = rel_bias.reshape(groups, GROUP * SLOT, SLOT)
    mask = jnp.asarray(region_mask())
    perm_host = token_permutation()
    perm = jnp.asarray(perm_host, BF16)
    back = jnp.asarray(perm_host.T, BF16)

    image_block = per_step(BATCH, GRID, GRID, width)
    shape = jax.ShapeDtypeStruct
    params = pltpu.CompilerParams(
        dimension_semantics=("arbitrary",), vmem_limit_bytes=60 * 1024 * 1024
    )
    tokens = number * ROWS
    output, mixed, attended, middle, probs, expand_grad, reduce_grad, sums, expand_sums = pl.pallas_call(
        functools.partial(forward_kernel, width_head),
        grid=(steps,),
        in_specs=[
            image_block, image_block, whole(weights.shape), whole(reduce.shape), whole(vectors.shape),
            whole(qkv_bias.shape), whole(expand_bias.shape), whole(rel_bias.shape), whole(mask.shape),
            whole(perm.shape), whole(back.shape),
        ],
        out_specs=[
            image_block, per_step(rows, 3 * width), per_step(rows, width), per_step(rows, width),
            per_step(windows * groups, GROUP * SLOT, SLOT),
            kept((width, hidden_width)), kept((hidden_width, width)), kept((8, width)),
            kept((1, hidden_width)),
        ],
        out_shape=[
            shape(images.shape, BF16), shape((tokens, 3 * width), BF16), shape((tokens, width), BF16),
            shape((tokens, width), F32),
            shape((number * ACROSS * ACROSS * groups, GROUP * SLOT, SLOT), BF16),
            shape((width, hidden_width), BF16), shape((hidden_width, width), BF16),
            shape((8, width), F32), shape((1, hidden_width), F32),
        ],
        scratch_shapes=[
            pltpu.VMEM((GRID * LINE, width), BF16), pltpu.VMEM((rows, width), F32),
            pltpu.VMEM((rows, width), F32), pltpu.VMEM((rows, 3 * width), F32),
            pltpu.VMEM((rows, width), F32), pltpu.VMEM((width, hidden_width), F32),
            pltpu.VMEM((hidden_width, width), F32),
        ],
        compiler_params=params,
        cost_estimate=pl.CostEstimate(flops=50 * 10**9, bytes_accessed=60 * 10**6, transcendentals=0),
    )(images, cotangent, weights, reduce, vectors, qkv_bias, expand_bias, rel_bias, mask, perm, back)

    expand_owned = reduce_owned(expand_grad)
    reduce_owned_grad = reduce_owned(reduce_grad)

    input_grad, weight_grad, sums_two, mixed_sums, rel_grad = pl.pallas_call(
        functools.partial(backward_kernel, width_head),
        grid=(steps,),
        in_specs=[
            image_block, whole((width, 4 * width)), whole(vectors.shape), per_step(rows, 3 * width),
            per_step(rows, width), per_step(rows, width),
            per_step(windows * groups, GROUP * SLOT, SLOT), whole(perm.shape), whole(back.shape),
        ],
        out_specs=[
            image_block, kept((width, 4 * width)), kept((8, width)), kept((1, 3 * width)),
            kept((groups, GROUP * SLOT, SLOT)),
        ],
        out_shape=[
            shape(images.shape, BF16), shape((width, 4 * width), BF16), shape((8, width), F32),
            shape((1, 3 * width), F32), shape((groups, GROUP * SLOT, SLOT), F32),
        ],
        scratch_shapes=[
            pltpu.VMEM((GRID * LINE, width), BF16), pltpu.VMEM((rows, width), F32),
            pltpu.VMEM((rows, 3 * width), F32), pltpu.VMEM((rows, width), F32),
            pltpu.VMEM((rows, 3 * width), F32), pltpu.VMEM((width, 4 * width), F32),
        ],
        compiler_params=params,
        cost_estimate=pl.CostEstimate(flops=30 * 10**9, bytes_accessed=60 * 10**6, transcendentals=0),
    )(images, weights, vectors, mixed, attended, middle, probs, perm, back)

    weight_owned = reduce_owned(weight_grad).astype(F32)

    rel_rows = rel_grad.reshape(heads, SLOT, SLOT)[:, :LEN, :LEN].reshape(heads, LEN * LEN)
    table_grad = lax.dot_general(
        rel_rows, hot.astype(F32), (((1,), (1,)), ((), ())), precision=lax.Precision.HIGHEST
    ).reshape(-1)
    lines = -(-table_grad.shape[0] // width)
    table_grad = jnp.pad(table_grad, (0, lines * width - table_grad.shape[0])).reshape(lines, width)
    mixed_lines = mixed_sums.reshape(3, width)
    packed = jnp.concatenate(
        [
            sums_two[1:2], sums[0:1], sums_two[2:3], sums[1:2], mixed_lines[0:1], mixed_lines[2:3],
            sums_two[0:1], sums[2:3], expand_sums.reshape(hidden_width // width, width), table_grad,
        ]
    )
    packed = lax.psum(packed, ("replica", "weight"))
    mine = lax.axis_index("weight")
    features = lax.dynamic_slice_in_dim(packed[:8], mine * own, own, axis=1)
    hidden_lines = hidden_width // width
    expand_bias_grad = lax.dynamic_slice_in_dim(
        packed[8 : 8 + hidden_lines].reshape(-1), mine * (hidden_width // shards), hidden_width // shards
    )
    table_grad = packed[8 + hidden_lines :].reshape(-1)[: heads * SPAN].reshape(heads, SPAN)
    table_grad = lax.dynamic_slice_in_dim(table_grad, mine * (heads // shards), heads // shards).T
    return (
        output,
        input_grad,
        features[:2],
        features[2:],
        weight_owned[:, : 3 * width],
        table_grad,
        weight_owned[:, 3 * width :],
        expand_owned.astype(F32),
        expand_bias_grad,
        reduce_owned_grad.astype(F32),
    )


def solution(mesh):
    in_specs = (
        P(("replica", "weight"), None, None, None),
        P(None, "weight"),
        P(None, "weight"),
        P("weight", None),
        P(None, "weight"),
        P("weight", None),
        P("weight", None),
        P("weight"),
        P("weight", None),
        P(),
        P(("replica", "weight"), None, None, None),
    )
    out_specs = (
        P(("replica", "weight"), None, None, None),
        P(("replica", "weight"), None, None, None),
        P(None, "weight"),
        P(None, "weight"),
        P("weight", None),
        P(None, "weight"),
        P("weight", None),
        P("weight", None),
        P("weight"),
        P("weight", None),
    )
    return jax.shard_map(
        functools.partial(per_device, mesh.shape["weight"]),
        mesh=mesh,
        in_specs=in_specs,
        out_specs=out_specs,
        check_vma=False,
    )
```

time: 995 us -> 509 us (0.51); the launches traced: 979 us -> 509 us
  matrix products: 303 us -> 1.68 us
  local copies, waits for them, and re-layouts: 319 us -> 28.1 us
  Pallas kernels: 0 us -> 228 us
  waiting for transfers between devices: 53.2 us -> 181 us
  blocking collectives: 174 us -> 47.4 us
  other arithmetic: 113 us -> 7.58 us
    dot_general x20 -> x2, matrix products: 303 us -> 1.68 us  [the longest x1 0.89 us: per_device(): lax.dot_general(rel_rows, hot.astype(F32), (((1,), (1,)), ((), ())), prec...]
    pallas_call x0 -> x2, Pallas kernels: none -> 228 us  [the longest x1 134 us: per_device(): pl.pallas_call(functools.partial(forward_kernel, width_head), grid=(steps...]
    convert_element_type x6 -> x0, local copies, waits for them, and re-layouts: 98.3 us -> none  [the longest x2 64.4 us: per_device(): grad_mixed = jnp.stack([grad_queries, grad_keys, grad_values], axis=2).re...]
    reduce_sum x12 -> x0, other arithmetic: 91 us -> none  [the longest x1 27.6 us: per_device(): jnp.sum(scores_low.astype(jnp.float32), axis=0).transpose(1, 2, 0)]
    psum x1, blocking collectives: 130 us -> 41.2 us  [per_device(): packed = lax.psum(packed, ('replica', 'weight'))]
    reshape x9, local copies, waits for them, and re-layouts: 71.7 us -> 0.59 us  [the longest x1 0.17 us: per_device(): rel_grad.reshape(heads, SLOT, SLOT)[:, :LEN, :LEN].reshape(heads, LEN * LEN)]
    unnamed x120 -> x33, local copies, waits for them, and re-layouts: 68.8 us -> 17.5 us
    reduce_scatter x4 -> x3, waiting for transfers between devices: 51 us -> 99.3 us  [reduce_owned(): mine = lax.psum_scatter(grad, 'weight', scatter_dimension=0, tiled=True)]
  transfers between devices with their start and end apart: 9 -> 6, of which waited for: 2 -> 6; matrix products, arithmetic and copies ran while one was open for 46% -> 6% of each run, Pallas kernels for 0% -> 0%
where the time goes in v1:
time: 509 us
  Pallas kernels  228 us (45%)
  waiting for transfers between devices  181 us (36%)
  blocking collectives  47.4 us (9%)
  local copies, waits for them, and re-layouts  28.1 us (6%)
  between operations  14.4 us (3%)
  other arithmetic  7.58 us (1%)
    pallas_call x1, Pallas kernels, per_device(): pl.pallas_call(functools.partial(forward_kernel, width_head), grid=(steps...  134 us
    reduce_scatter x3, waiting for transfers between devices, reduce_owned(): mine = lax.psum_scatter(grad, 'weight', scatter_dimension=0, tiled=True)  99.3 us
    pallas_call x1, Pallas kernels, per_device(): pl.pallas_call(functools.partial(backward_kernel, width_head), grid=(step...  94.5 us
    psum x1, blocking collectives, per_device(): packed = lax.psum(packed, ('replica', 'weight'))  41.2 us
    psum x1, waiting for transfers between devices, reduce_owned(): return lax.psum(mine, 'replica')  36.9 us
    all_gather x1, waiting for transfers between devices, per_device(): lax.all_gather(jnp.concatenate([qkv_weight, proj_weight, fc1_weight], axi...  36.6 us
    unnamed x33, local copies, waits for them, and re-layouts  17.5 us
  transfers between devices with their start and end apart: 6, of which 6 were waited for; matrix products, arithmetic and copies ran while one was open for 6% of the time, Pallas kernels for 0%

profile of v1, /device:TPU:0, one launch (start us, length us, event | category | flops | bytes accessed | tf_op | source)
XLA Modules:
  0.0 508.9 jit_solution(17363631415868760500)
XLA Ops:
  7.3 0.7 all-gather.7.cloned.1.call-update
  8.0 2.5 pad_maximum_fusion
  10.7 6.2 %all-gather.1 = bf16[4,18,128]{2,1,0:T(8,128)(2,1)S(1)} all-gather(bf16[1,18,128]{2,1,0:T(8,128)(2,1)S(1)} %maximum_bitcast_fusion), channel_id=2, replica_groups=mesh['replica'=8,'weight'=4] {'weight'}, dimensions={0}, use_global_device_ids=true | all-gather | bytes 23040 | tf_op jit(solution)/shard_map/all_gather | solution.py:327
  17.0 0.6 convert_bitcast_fusion.1
  17.6 0.6 broadcast_in_dim.8.qkv_bias
  18.3 0.8 fusion.1
  19.3 0.8 pad.13.clone
  20.1 3.8 copy.41.images
  23.8 3.7 copy.42.cotangent
  27.5 0.6 slice_convert_fusion
  28.1 6.8 %all-gather.7.cloned.1.call-done.reduce = bf16[2048,512]{1,0:T(8,128)(2,1)} async-done(((bf16[512,512]{1,0:T(8,128)(2,1)}), bf16[2048,512]{1,0:T(8,128)(2,1)}) %all-gather.7.cloned.1.call-update) | async-done | bytes 2097168 | tf_op jit(solution)/shard_map/all_gather | solution.py:319
  35.0 36.6 %all-gather.5.cloned.1.call-done.weights = bf16[512,4096]{1,0:T(8,128)(2,1)} async-done(((bf16[128,4096]{1,0:T(8,128)(2,1)}), bf16[512,4096]{1,0:T(8,128)(2,1)}) %all-gather.5.cloned.1.call-update) | async-done | bytes 4194320 | tf_op jit(solution)/shard_map/all_gather | solution.py:316
  71.6 133.6 %shard_map.213 = (bf16[16,14,14,512]{3,2,1,0:T(8,128)(2,1)}, bf16[3584,1536]{1,0:T(8,128)(2,1)}, bf16[3584,512]{1,0:T(8,128)(2,1)}, f32[3584,512]{1,0:T(8,128)},...) custom-call(bf16[16,14,14,512]{3,2,1,0:T(8,128)(2,1)} %copy.41.image, ...), custom_call_target="tpu_custom_call" | custom-call | flops 49999998976 | bytes 60000000 | tf_op jit(solution)/shard_map/pallas_call | solution.py:350
  205.2 94.5 %shard_map.214 = (bf16[16,14,14,512]{3,2,1,0:T(8,128)(2,1)}, bf16[512,2048]{1,0:T(8,128)(2,1)}, f32[8,512]{1,0:T(8,128)}, f32[1,1536]{1,0:T(1,128)}, f32[4,224,56]{2,1,0:T(8,128)}) custom-call(bf16[16,14,14,512]{3,2,1,0:T(8,128)(2,1)} %copy.41.images, bf16[512,4096]{1,0:T(8,128)(2,1)} %all-gather.5.cloned.1.call-done.weights, ...), custom_call_target="tpu_custom_call" | custom-call | flops 30000001024 | bytes 60000000 | tf_op jit(solution)/shard_map/pallas_call | solution.py:384
  301.0 30.3 %reduce-scatter.4.cloned.1.call-done = bf16[128,2048]{1,0:T(8,128)(2,1)} async-done(((bf16[512,2048]{1,0:T(8,128)(2,1)}), bf16[128,2048]{1,0:T(8,128)(2,1)}) %reduce-scatter.4.cloned.1.call-update) | async-done | bytes 524304 | tf_op jit(solution)/shard_map/reduce_scatter | solution.py:298
  331.3 34.6 %reduce-scatter.6.cloned.1.call-done = bf16[128,2048]{1,0:T(8,128)(2,1)} async-done(((bf16[512,2048]{1,0:T(8,128)(2,1)}), bf16[128,2048]{1,0:T(8,128)(2,1)}) %reduce-scatter.6.cloned.1.call-update) | async-done | bytes 524304 | tf_op jit(solution)/shard_map/reduce_scatter | solution.py:298
  365.9 34.4 %reduce-scatter.8.cloned.1.call-done = bf16[512,512]{1,0:T(8,128)(2,1)} async-done(((bf16[2048,512]{1,0:T(8,128)(2,1)}), bf16[512,512]{1,0:T(8,128)(2,1)}) %reduce-scatter.8.cloned.1.call-update) | async-done | bytes 524304 | tf_op jit(solution)/shard_map/reduce_scatter | solution.py:298
  401.0 0.7 reduce.3
  401.8 0.9 fusion.3
  402.9 0.8 fusion.6
  403.7 0.8 fusion.7
  404.7 41.2 %psum.28 = f32[18,512]{1,0:T(8,128)S(1)} all-reduce(f32[18,512]{1,0:T(8,128)S(1)} %concatenate.15), channel_id=1, replica_groups=mesh['replica'=8,'weight'=4] {'replica','weight'}, use_global_device_ids=true, to_apply=%region_0.1 | all-reduce | flops 9216 | bytes 73728 | tf_op jit(solution)/shard_map/psum | solution.py:424
  446.5 0.6 slice.90
  447.1 6.0 %copy.45 = bf16[16,14,14,512]{3,0,2,1:T(8,128)(2,1)} copy(bf16[16,14,14,512]{3,2,1,0:T(8,128)(2,1)} %get-tuple-element.58) | data formatting | bytes 6422528
  453.1 3.8 copy.46
  457.1 0.7 dynamic_slice.11
  457.7 0.6 dynamic-slice_bitcast_fusion
  458.3 36.9 %all-reduce.6.cloned.1.call-done = (bf16[128,2048]{1,0:T(8,128)(2,1)}, bf16[128,2048]{1,0:T(8,128)(2,1)}, bf16[512,512]{1,0:T(8,128)(2,1)}) async-done(((bf16[128,2048]{1,0:T(8,128)(2,1)}, bf16[128,2048]{1,0:T(8,128)(2,1)}, bf16[512,512]{1,0:T(8,128)(2,1)}), (bf16[128,2048]{1,0:T(8,128)(2,1)}, bf16[128,2048]{1,0:T(8,128)(2,1)}, bf16[512,512]{1,0:T(8,128)(2,1)})) %all-reduce.6.cloned.1.call-update) | async-done | bytes 1572880 | tf_op jit(solution)/shard_map/psum | solution.py:299
  495.2 1.7 slice.107
  496.9 2.0 slice.104
  498.8 2.1 convert_element_type.35
  500.9 1.1 convert_element_type.36
  (62 shorter events, 3.6 us)
Async XLA Ops:
  7.2 3.4 copy-start.8
  7.2 3.5 copy-start.10
  7.2 3.5 copy-start.9
  7.2 3.5 copy-start.11
  7.2 11.0 %copy-start.5 = (s32[49,49]{1,0:T(8,128)S(1)}, s32[49,49]{1,0:T(8,128)}, u32[]{:S(2)}) copy-start(s32[49,49]{1,0:T(8,128)} %param.23) | copy-start | bytes 28816
  7.2 12.8 %copy-start.1 = (bf16[16,14,14,512]{3,0,2,1:T(8,128)(2,1)S(1)}, bf16[16,14,14,512]{3,0,2,1:T(8,128)(2,1)}, u32[]{:S(2)}) copy-start(bf16[16,14,14,512]{3,0,2,1:T(8,128)(2,1)} %param.14) | copy-start | bytes 9633796
  7.2 27.7 %all-gather.7.cloned.1.call-start = ((), (), s32[]{:S(2)}) async-start(), calls=%async_computation.4 | async-start | bytes 2621440 | tf_op jit(solution)/shard_map/all_gather | solution.py:319
  8.0 63.6 %all-gather.5.cloned.1.call-start = ((), (), s32[]{:S(2)}) async-start(), calls=%async_computation.3 | async-start | bytes 5242880 | tf_op jit(solution)/shard_map/all_gather | solution.py:316
  10.5 320.8 %reduce-scatter.4.cloned.1.call-start = ((), (), s32[]{:S(2)}) async-start(), calls=%async_computation.5 | async-start | bytes 2621440 | tf_op jit(solution)/shard_map/reduce_scatter | solution.py:298
  20.1 3.8 copy-start.2
  299.7 101.2 %copy-start.6 = (f32[1,2048]{1,0:T(1,128)S(1)}, f32[1,2048]{1,0:T(1,128)}, u32[]{:S(2)}) copy-start(f32[1,2048]{1,0:T(1,128)} %get-tuple-element.33) | copy-start | bytes 24580
  299.7 101.9 %copy-start.4 = (f32[4,224,56]{2,1,0:T(8,128)S(1)}, f32[4,224,56]{2,1,0:T(8,128)}, u32[]{:S(2)}) copy-start(f32[4,224,56]{2,1,0:T(8,128)} %get-tuple-element.34) | copy-start | bytes 602116
  299.7 66.1 %reduce-scatter.6.cloned.1.call-start = ((), (), s32[]{:S(2)}) async-start(), calls=%async_computation.6 | async-start | bytes 2621440 | tf_op jit(solution)/shard_map/reduce_scatter | solution.py:298
  299.8 103.9 %copy-start.7 = (f32[1,1536]{1,0:T(1,128)S(1)}, f32[1,1536]{1,0:T(1,128)}, u32[]{:S(2)}) copy-start(f32[1,1536]{1,0:T(1,128)} %get-tuple-element.32) | copy-start | bytes 18436
  300.3 100.0 %reduce-scatter.8.cloned.1.call-start = ((), (), s32[]{:S(2)}) async-start(), calls=%async_computation.7 | async-start | bytes 2621440 | tf_op jit(solution)/shard_map/reduce_scatter | solution.py:298
  300.9 194.3 %all-reduce.6.cloned.1.call-start = ((), (), s32[]{:S(2)}) async-start(), calls=%async_computation.8 | async-start | bytes 3145728 | tf_op jit(solution)/shard_map/psum | solution.py:299
  447.1 6.0 %copy-start = (bf16[16,14,14,512]{3,2,1,0:T(8,128)(2,1)S(1)}, bf16[16,14,14,512]{3,2,1,0:T(8,128)(2,1)}, u32[]{:S(2)}) copy-start(bf16[16,14,14,512]{3,2,1,0:T(8,128)(2,1)} %get-tuple-element.59) | copy-start | bytes 9633796
  495.2 5.8 %copy-start.3 = (bf16[512,512]{1,0:T(8,128)(2,1)S(1)}, bf16[512,512]{1,0:T(8,128)(2,1)}, u32[]{:S(2)}) copy-start(bf16[512,512]{1,0:T(8,128)(2,1)} %get-tuple-element.70) | copy-start | bytes 1572868
Sparse Core Ops, SparseCore 0:
  9.6 25.2 all-gather.6
  37.1 34.4 all-gather.4
  299.8 31.4 reduce-scatter.3
  334.4 31.4 reduce-scatter.5
  368.8 31.4 reduce-scatter.7
  404.5 90.6 all-reduce.5

commit v2 on v1

--- a/solution.py
+++ b/solution.py
@@ -19,6 +19,7 @@
 SPAN = (2 * WIN - 1) ** 2
 GROUP = 4
 BATCH = 2
+UNROLL = 2
 F32 = jnp.float32
 BF16 = jnp.bfloat16
 EPSILON = 1e-05
@@ -127,30 +128,23 @@
         ref[at, r] = lines[r * LINE : r * LINE + GRID]
 
 
-def forward_kernel(
+def attention_kernel(
     width_head,
-    images, cotangent, weights, reduce, vectors, qkv_bias, expand_bias, rel_bias, mask, perm, back,
-    output, mixed_out, attended_out, middle_out, probs_out, expand_grad, reduce_grad, sums, expand_sums,
-    grid_rows, inputs, ups, mixed, attended, expand_acc, reduce_acc,
+    images, qkv_weight, vectors, qkv_bias, rel_bias, mask, perm,
+    mixed_out, attended_out, probs_out,
+    grid_rows, inputs, mixed, attended,
 ):
     width = inputs.shape[1]
-    hidden_width = expand_bias.shape[1]
-    step = pl.program_id(0)
-
-    @pl.when(step == 0)
+
+    @pl.when(pl.program_id(0) == 0)
     def _():
         grid_rows[...] = jnp.zeros_like(grid_rows)
-        expand_acc[...] = jnp.zeros_like(expand_acc)
-        reduce_acc[...] = jnp.zeros_like(reduce_acc)
-        sums[...] = jnp.zeros_like(sums)
-        expand_sums[...] = jnp.zeros_like(expand_sums)
 
     for b in range(BATCH):
         inputs[b * ROWS : (b + 1) * ROWS, :] = read_image(images, b, grid_rows, perm)
-        ups[b * ROWS : (b + 1) * ROWS, :] = read_image(cotangent, b, grid_rows, perm)
     unit, _ = normalise(inputs[...])
     normed = (unit * vectors[0:1, :] + vectors[2:3, :]).astype(BF16)
-    mixed_low = (dot(normed, weights[:, : 3 * width]) + qkv_bias[...]).astype(BF16)
+    mixed_low = (dot(normed, qkv_weight[...]) + qkv_bias[...]).astype(BF16)
     mixed_out[...] = mixed_low
     mixed[...] = mixed_low.astype(F32)
     scale = width_head ** (-0.5)
@@ -173,11 +167,30 @@
             attended[rows, g * size : (g + 1) * size] = t_dot(probs, values)
         return carry
 
-    lax.fori_loop(0, BATCH * ACROSS * ACROSS, attend, 0)
-
-    attended_low = attended[...].astype(BF16)
-    attended_out[...] = attended_low
-    middle = inputs[...] + dot(attended_low, weights[:, 3 * width : 4 * width]) + vectors[6:7, :]
+    lax.fori_loop(0, BATCH * ACROSS * ACROSS, attend, 0, unroll=UNROLL)
+    attended_out[...] = attended[...].astype(BF16)
+
+
+def mlp_kernel(
+    images, cotangent, attended, later, reduce, vectors, expand_bias, perm, back,
+    output, middle_out, expand_grad, reduce_grad, sums, expand_sums,
+    grid_rows, inputs, ups, expand_acc, reduce_acc,
+):
+    hidden_width = expand_bias.shape[1]
+    step = pl.program_id(0)
+
+    @pl.when(step == 0)
+    def _():
+        grid_rows[...] = jnp.zeros_like(grid_rows)
+        expand_acc[...] = jnp.zeros_like(expand_acc)
+        reduce_acc[...] = jnp.zeros_like(reduce_acc)
+        sums[...] = jnp.zeros_like(sums)
+        expand_sums[...] = jnp.zeros_like(expand_sums)
+
+    for b in range(BATCH):
+        inputs[b * ROWS : (b + 1) * ROWS, :] = read_image(images, b, grid_rows, perm)
+        ups[b * ROWS : (b + 1) * ROWS, :] = read_image(cotangent, b, grid_rows, perm)
+    middle = inputs[...] + dot(attended[...], later[:, hidden_width:]) + vectors[6:7, :]
     unit, inverse = normalise(middle)
     normed_two = (unit * vectors[1:2, :] + vectors[3:4, :]).astype(BF16)
     up = ups[...]
@@ -187,7 +200,7 @@
     chunk = 512
     for c in range(hidden_width // chunk):
         part = slice(c * chunk, (c + 1) * chunk)
-        expand_part = weights[:, 4 * width + c * chunk : 4 * width + (c + 1) * chunk]
+        expand_part = later[:, part]
         hidden = dot(normed_two, expand_part) + expand_bias[:, part]
         below, density = gelu_parts(hidden)
         activated = (hidden * below).astype(BF16)
@@ -214,7 +227,7 @@
 
 def backward_kernel(
     width_head,
-    images, weights, vectors, mixed_in, attended_in, middle_in, probs_in, perm, back,
+    images, qkv_weight, proj_weight, vectors, mixed_in, attended_in, middle_in, probs_in, perm, back,
     input_grad, weight_grad, sums, mixed_sums, rel_grad,
     grid_rows, inputs, mixed, grad_attended, grad_mixed, weight_acc,
 ):
@@ -235,7 +248,7 @@
     middle_low = middle_in[...].astype(BF16)
     weight_acc[:, 3 * width :] += t_dot(attended_in[...], middle_low)
     sums[0:1, :] += column_sum(middle_low.astype(F32))
-    grad_attended[...] = dot_t(middle_low, weights[:, 3 * width :]).astype(BF16).astype(F32)
+    grad_attended[...] = dot_t(middle_low, proj_weight[...]).astype(BF16).astype(F32)
     scale = width_head ** (-0.5)
 
     def attend(w, carry):
@@ -262,14 +275,14 @@
             grad_mixed[rows, 2 * width + g * size : 2 * width + (g + 1) * size] = grad_values
         return carry
 
-    lax.fori_loop(0, BATCH * ACROSS * ACROSS, attend, 0)
+    lax.fori_loop(0, BATCH * ACROSS * ACROSS, attend, 0, unroll=UNROLL)
 
     grad_low = grad_mixed[...].astype(BF16)
     mixed_sums[...] += column_sum(grad_low.astype(F32))
     unit, inverse = normalise(inputs[...])
     normed = (unit * vectors[0:1, :] + vectors[2:3, :]).astype(BF16)
     weight_acc[:, : 3 * width] += t_dot(normed, grad_low)
-    grad_normed = dot_t(grad_low, weights[:, : 3 * width])
+    grad_normed = dot_t(grad_low, qkv_weight[...])
     sums[1:2, :] += column_sum(grad_normed * unit)
     sums[2:3, :] += column_sum(grad_normed)
     total = middle_in[...] + norm_back(grad_normed, unit, inverse, vectors[0:1, :])
@@ -279,7 +292,7 @@
 
     @pl.when(step == pl.num_programs(0) - 1)
     def _():
-        weight_grad[...] = weight_acc[...].astype(BF16)
+        weight_grad[:, : 4 * width] = weight_acc[...].astype(BF16)
 
 
 def whole(shape):
@@ -295,8 +308,7 @@
 
 
 def reduce_owned(grad):
-    mine = lax.psum_scatter(grad, "weight", scatter_dimension=0, tiled=True)
-    return lax.psum(mine, "replica")
+    return lax.psum_scatter(grad, "weight", scatter_dimension=0, tiled=True)
 
 
 def per_device(
@@ -313,10 +325,7 @@
     rows = BATCH * ROWS
     windows = BATCH * ACROSS * ACROSS
 
-    weights = lax.all_gather(
-        jnp.concatenate([qkv_weight, proj_weight, fc1_weight], axis=1), "weight", axis=0, tiled=True
-    )
-    reduce = lax.all_gather(fc2_weight, "weight", axis=0, tiled=True)
+    qkv_full = lax.all_gather(qkv_weight, "weight", axis=0, tiled=True)
     hidden_lines = hidden_width // shards // own
     table_own = bias_table.T.reshape(-1)
     table_lines = -(-table_own.shape[0] // own)
@@ -336,6 +345,12 @@
     rel_bias = dot(table, hot).reshape(heads, LEN, LEN)
     rel_bias = jnp.pad(rel_bias, ((0, 0), (0, SLOT - LEN), (0, SLOT - LEN)))
     rel_bias = rel_bias.reshape(groups, GROUP * SLOT, SLOT)
+    later = jnp.concatenate([fc1_weight, proj_weight], axis=1)
+    qkv_full, vectors, expand_bias, rel_bias, later, fc2_weight = lax.optimization_barrier(
+        (qkv_full, vectors, expand_bias, rel_bias, later, fc2_weight)
+    )
+    later = lax.all_gather(later, "weight", axis=0, tiled=True)
+    reduce = lax.all_gather(fc2_weight, "weight", axis=0, tiled=True)
     mask = jnp.asarray(region_mask())
     perm_host = token_permutation()
     perm = jnp.asarray(perm_host, BF16)
@@ -347,54 +362,74 @@
         dimension_semantics=("arbitrary",), vmem_limit_bytes=60 * 1024 * 1024
     )
     tokens = number * ROWS
-    output, mixed, attended, middle, probs, expand_grad, reduce_grad, sums, expand_sums = pl.pallas_call(
-        functools.partial(forward_kernel, width_head),
+    mixed, attended, probs = pl.pallas_call(
+        functools.partial(attention_kernel, width_head),
         grid=(steps,),
         in_specs=[
-            image_block, image_block, whole(weights.shape), whole(reduce.shape), whole(vectors.shape),
-            whole(qkv_bias.shape), whole(expand_bias.shape), whole(rel_bias.shape), whole(mask.shape),
-            whole(perm.shape), whole(back.shape),
+            image_block, whole(qkv_full.shape), whole(vectors.shape), whole(qkv_bias.shape),
+            whole(rel_bias.shape), whole(mask.shape), whole(perm.shape),
         ],
         out_specs=[
-            image_block, per_step(rows, 3 * width), per_step(rows, width), per_step(rows, width),
+            per_step(rows, 3 * width), per_step(rows, width),
             per_step(windows * groups, GROUP * SLOT, SLOT),
-            kept((width, hidden_width)), kept((hidden_width, width)), kept((8, width)),
-            kept((1, hidden_width)),
         ],
         out_shape=[
-            shape(images.shape, BF16), shape((tokens, 3 * width), BF16), shape((tokens, width), BF16),
-            shape((tokens, width), F32),
+            shape((tokens, 3 * width), BF16), shape((tokens, width), BF16),
             shape((number * ACROSS * ACROSS * groups, GROUP * SLOT, SLOT), BF16),
+        ],
+        scratch_shapes=[
+            pltpu.VMEM((GRID * LINE, width), BF16), pltpu.VMEM((rows, width), F32),
+            pltpu.VMEM((rows, 3 * width), F32), pltpu.VMEM((rows, width), F32),
+        ],
+        compiler_params=params,
+        cost_estimate=pl.CostEstimate(flops=60 * 10**9, bytes_accessed=40 * 10**6, transcendentals=0),
+    )(images, qkv_full, vectors, qkv_bias, rel_bias, mask, perm)
+
+    output, middle, expand_grad, reduce_grad, sums, expand_sums = pl.pallas_call(
+        mlp_kernel,
+        grid=(steps,),
+        in_specs=[
+            image_block, image_block, per_step(rows, width), whole(later.shape), whole(reduce.shape), whole(vectors.shape),
+            whole(expand_bias.shape), whole(perm.shape), whole(back.shape),
+        ],
+        out_specs=[
+            image_block, per_step(rows, width), kept((width, hidden_width)),
+            kept((hidden_width, width)), kept((8, width)), kept((1, hidden_width)),
+        ],
+        out_shape=[
+            shape(images.shape, BF16), shape((tokens, width), F32),
             shape((width, hidden_width), BF16), shape((hidden_width, width), BF16),
             shape((8, width), F32), shape((1, hidden_width), F32),
         ],
         scratch_shapes=[
             pltpu.VMEM((GRID * LINE, width), BF16), pltpu.VMEM((rows, width), F32),
-            pltpu.VMEM((rows, width), F32), pltpu.VMEM((rows, 3 * width), F32),
             pltpu.VMEM((rows, width), F32), pltpu.VMEM((width, hidden_width), F32),
             pltpu.VMEM((hidden_width, width), F32),
         ],
         compiler_params=params,
-        cost_estimate=pl.CostEstimate(flops=50 * 10**9, bytes_accessed=60 * 10**6, transcendentals=0),
-    )(images, cotangent, weights, reduce, vectors, qkv_bias, expand_bias, rel_bias, mask, perm, back)
+        cost_estimate=pl.CostEstimate(flops=70 * 10**9, bytes_accessed=40 * 10**6, transcendentals=0),
+    )(images, cotangent, attended, later, reduce, vectors, expand_bias, perm, back)
 
     expand_owned = reduce_owned(expand_grad)
     reduce_owned_grad = reduce_owned(reduce_grad)
+    proj_block = pl.BlockSpec(
+        (width, width), lambda i: (0, hidden_width // width), pipeline_mode=pl.Buffered(1)
+    )
 
     input_grad, weight_grad, sums_two, mixed_sums, rel_grad = pl.pallas_call(
         functools.partial(backward_kernel, width_head),
         grid=(steps,),
         in_specs=[
-            image_block, whole((width, 4 * width)), whole(vectors.shape), per_step(rows, 3 * width),
-            per_step(rows, width), per_step(rows, width),
+            image_block, whole(qkv_full.shape), proj_block, whole(vectors.shape),
+            per_step(rows, 3 * width), per_step(rows, width), per_step(rows, width),
             per_step(windows * groups, GROUP * SLOT, SLOT), whole(perm.shape), whole(back.shape),
         ],
         out_specs=[
-            image_block, kept((width, 4 * width)), kept((8, width)), kept((1, 3 * width)),
+            image_block, kept((width, 4 * width + own)), kept((8, width)), kept((1, 3 * width)),
             kept((groups, GROUP * SLOT, SLOT)),
         ],
         out_shape=[
-            shape(images.shape, BF16), shape((width, 4 * width), BF16), shape((8, width), F32),
+            shape(images.shape, BF16), shape((width, 4 * width + own), BF16), shape((8, width), F32),
             shape((1, 3 * width), F32), shape((groups, GROUP * SLOT, SLOT), F32),
         ],
         scratch_shapes=[
@@ -403,43 +438,53 @@
             pltpu.VMEM((rows, 3 * width), F32), pltpu.VMEM((width, 4 * width), F32),
         ],
         compiler_params=params,
-        cost_estimate=pl.CostEstimate(flops=30 * 10**9, bytes_accessed=60 * 10**6, transcendentals=0),
-    )(images, weights, vectors, mixed, attended, middle, probs, perm, back)
-
-    weight_owned = reduce_owned(weight_grad).astype(F32)
+        cost_estimate=pl.CostEstimate(flops=110 * 10**9, bytes_accessed=60 * 10**6, transcendentals=0),
+    )(images, qkv_full, later, vectors, mixed, attended, middle, probs, perm, back)
 
     rel_rows = rel_grad.reshape(heads, SLOT, SLOT)[:, :LEN, :LEN].reshape(heads, LEN * LEN)
     table_grad = lax.dot_general(
         rel_rows, hot.astype(F32), (((1,), (1,)), ((), ())), precision=lax.Precision.HIGHEST
-    ).reshape(-1)
-    lines = -(-table_grad.shape[0] // width)
-    table_grad = jnp.pad(table_grad, (0, lines * width - table_grad.shape[0])).reshape(lines, width)
+    ).reshape(shards, table_own.shape[0])
+    table_grad = jnp.pad(table_grad, ((0, 0), (0, table_lines * own - table_own.shape[0])))
     mixed_lines = mixed_sums.reshape(3, width)
-    packed = jnp.concatenate(
+    features = jnp.concatenate(
         [
             sums_two[1:2], sums[0:1], sums_two[2:3], sums[1:2], mixed_lines[0:1], mixed_lines[2:3],
-            sums_two[0:1], sums[2:3], expand_sums.reshape(hidden_width // width, width), table_grad,
+            sums_two[0:1], sums[2:3],
         ]
     )
-    packed = lax.psum(packed, ("replica", "weight"))
-    mine = lax.axis_index("weight")
-    features = lax.dynamic_slice_in_dim(packed[:8], mine * own, own, axis=1)
-    hidden_lines = hidden_width // width
-    expand_bias_grad = lax.dynamic_slice_in_dim(
-        packed[8 : 8 + hidden_lines].reshape(-1), mine * (hidden_width // shards), hidden_width // shards
-    )
-    table_grad = packed[8 + hidden_lines :].reshape(-1)[: heads * SPAN].reshape(heads, SPAN)
-    table_grad = lax.dynamic_slice_in_dim(table_grad, mine * (heads // shards), heads // shards).T
+    small_grad = jnp.concatenate(
+        [
+            features.reshape(8, shards, own).transpose(1, 0, 2),
+            expand_sums.reshape(shards, hidden_lines, own),
+            table_grad.reshape(shards, table_lines, own),
+        ],
+        axis=1,
+    )
+    small_grad = jnp.pad(small_grad, ((0, 0), (0, own - small_grad.shape[1]), (0, 0)))
+    weight_grad = lax.dynamic_update_slice(
+        weight_grad, small_grad.reshape(width, own).astype(BF16), (0, 4 * width)
+    )
+    weight_grad, expand_owned, reduce_owned_grad = lax.optimization_barrier(
+        (weight_grad, expand_owned, reduce_owned_grad)
+    )
+    weight_owned, expand_owned, reduce_owned_grad = lax.psum(
+        (reduce_owned(weight_grad), expand_owned, reduce_owned_grad), "replica"
+    )
+    weight_owned = weight_owned.astype(F32)
+    small_owned = weight_owned[:, 4 * width :]
+    table_grad = small_owned[8 + hidden_lines : 8 + hidden_lines + table_lines].reshape(-1)
+    table_grad = table_grad[: table_own.shape[0]].reshape(-1, SPAN).T
     return (
         output,
         input_grad,
-        features[:2],
-        features[2:],
+        small_owned[:2],
+        small_owned[2:8],
         weight_owned[:, : 3 * width],
         table_grad,
-        weight_owned[:, 3 * width :],
+        weight_owned[:, 3 * width : 4 * width],
         expand_owned.astype(F32),
-        expand_bias_grad,
+        small_owned[8 : 8 + hidden_lines].reshape(-1),
         reduce_owned_grad.astype(F32),
     )
 

time: 509 us -> 407 us (0.80)
  waiting for transfers between devices: 181 us -> 132 us
  blocking collectives: 47.4 us -> 6.19 us
  Pallas kernels: 228 us -> 213 us
    reduce_scatter x3, waiting for transfers between devices: 99.3 us -> 32.4 us  [reduce_owned(): return lax.psum_scatter(grad, 'weight', scatter_dimension=0, tiled=True)]
    psum x1, waiting for transfers between devices: 36.9 us -> 85.7 us  [per_device(): lax.psum((reduce_owned(weight_grad), expand_owned, reduce_owned_grad), 'r...]
    psum x1 -> x0, blocking collectives: 41.2 us -> none  [per_device(): packed = lax.psum(packed, ('replica', 'weight'))]
    all_gather x1 -> x2, waiting for transfers between devices: 36.6 us -> 12.9 us  [the longest x1 10.5 us: per_device(): qkv_full = lax.all_gather(qkv_weight, 'weight', axis=0, tiled=True)]
    pallas_call x1, Pallas kernels: 94.5 us -> 85.1 us  [per_device(): pl.pallas_call(functools.partial(backward_kernel, width_head), grid=(step...]
    all_gather x1, waiting for transfers between devices: 6.85 us -> 0.01 us  [per_device(): reduce = lax.all_gather(fc2_weight, 'weight', axis=0, tiled=True)]
    pallas_call x1 -> x2, Pallas kernels: 134 us -> 128 us  [the longest x1 86.7 us: per_device(): pl.pallas_call(mlp_kernel, grid=(steps,), in_specs=[image_block, image_bl...]
    unnamed x33 -> x31, local copies, waits for them, and re-layouts: 17.5 us -> 17.5 us
  transfers between devices with their start and end apart: 6 -> 7, of which waited for: 6 -> 4; matrix products, arithmetic and copies ran while one was open for 6% -> 7% of each run, Pallas kernels for 0% -> 31%
where the time goes in v2:
time: 407 us
  Pallas kernels  213 us (52%)
  waiting for transfers between devices  132 us (32%)
  local copies, waits for them, and re-layouts  30.2 us (7%)
  between operations  14.3 us (4%)
  other arithmetic  8.73 us (2%)
  blocking collectives  6.19 us (2%)
    pallas_call x1, Pallas kernels, per_device(): pl.pallas_call(mlp_kernel, grid=(steps,), in_specs=[image_block, image_bl...  86.7 us
    psum x1, waiting for transfers between devices, per_device(): lax.psum((reduce_owned(weight_grad), expand_owned, reduce_owned_grad), 'r...  85.7 us
    pallas_call x1, Pallas kernels, per_device(): pl.pallas_call(functools.partial(backward_kernel, width_head), grid=(step...  85.1 us
    pallas_call x1, Pallas kernels, per_device(): pl.pallas_call(functools.partial(attention_kernel, width_head), grid=(ste...  41.1 us
    reduce_scatter x3, waiting for transfers between devices, reduce_owned(): return lax.psum_scatter(grad, 'weight', scatter_dimension=0, tiled=True)  32.4 us
    unnamed x31, local copies, waits for them, and re-layouts  17.5 us
    all_gather x1, waiting for transfers between devices, per_device(): qkv_full = lax.all_gather(qkv_weight, 'weight', axis=0, tiled=True)  10.5 us
  transfers between devices with their start and end apart: 7, of which 4 were waited for; matrix products, arithmetic and copies ran while one was open for 7% of the time, Pallas kernels for 31%

profile of v2, /device:TPU:0, one launch (start us, length us, event | category | flops | bytes accessed | tf_op | source)
XLA Modules:
  0.0 406.9 jit_solution(10867086090163086543)
XLA Ops:
  7.2 0.7 all-gather.6.cloned.1.call-update
  8.0 0.8 reshape.129
  8.7 0.7 maximum_bitcast_fusion
  9.5 6.2 %all-gather.1 = bf16[4,18,128]{2,1,0:T(8,128)(2,1)S(1)} all-gather(bf16[1,18,128]{2,1,0:T(8,128)(2,1)S(1)} %maximum_bitcast_fusion), channel_id=2, replica_groups=mesh['replica'=8,'weight'=4] {'weight'}, dimensions={0}, use_global_device_ids=true | all-gather | bytes 23040 | tf_op jit(solution)/shard_map/all_gather | solution.py:336
  15.8 0.8 copy.45
  16.6 0.8 fusion.1
  17.5 0.8 pad.19.clone
  19.5 2.0 pad_maximum_fusion
  21.5 10.5 %all-gather.6.cloned.1.call-done.qkv_weight = bf16[512,1536]{1,0:T(8,128)(2,1)} async-done(((bf16[128,1536]{1,0:T(8,128)(2,1)}), bf16[512,1536]{1,0:T(8,128)(2,1)}) %all-gather.6.cloned.1.call-update) | async-done | bytes 1572880 | tf_op jit(solution)/shard_map/all_gather | solution.py:328
  32.1 3.6 copy.48.images
  35.7 3.8 copy.49.cotangent
  40.3 41.1 %shard_map.213 = (bf16[3584,1536]{1,0:T(8,128)(2,1)}, bf16[3584,512]{1,0:T(8,128)(2,1)}, bf16[256,224,56]{2,1,0:T(8,128)(2,1)}) custom-call(bf16[16,14,14,512]{3,2,1,0:T(8,128)(2,1)} %copy.48.images, bf16[512,1536]{1,0:T(8,128)(2,1)} %all-gather.6.cloned.1.call-done.qkv_weight, f32[8,512]{1,0:T(8,128)} %get-tuple-element.34.vectors, ...), custom_call_target="tpu_custom_call" | custom-call | flops 60000002048 | bytes 40000000 | tf_op jit(solution)/shard_map/pallas_call | solution.py:365
  81.5 2.4 all-gather.8.cloned.1.call-done.later.proj_weight
  83.9 86.7 %shard_map.214 = (bf16[16,14,14,512]{3,2,1,0:T(8,128)(2,1)}, f32[3584,512]{1,0:T(8,128)}, bf16[512,2048]{1,0:T(8,128)(2,1)}, bf16[2048,512]{1,0:T(8,128)(2,1)}, f32[8,512]{1,0:T(8,128)}, /*index=5*/f32[1,2048]{1,0:T(1,128)}) custom-call(bf16[16,14,14,512]{3,2,1,0:T(8,128)(2,1)} %copy.48.images, bf16[16,14,14,512]{3,2,1,0:T(8,128)(2,1)} %copy.49.cotangent, ...), custom_call_target="tpu_custom_call" | custom-call | flops 70000001024 | bytes 40000000 | tf_op jit(solution)/shard_map/pallas_call | solution.py:388
  171.5 85.1 %shard_map.215 = (bf16[16,14,14,512]{3,2,1,0:T(8,128)(2,1)}, bf16[512,2176]{1,0:T(8,128)(2,1)}, f32[8,512]{1,0:T(8,128)}, f32[1,1536]{1,0:T(1,128)}, f32[4,224,56]{2,1,0:T(8,128)}) custom-call(bf16[16,14,14,512]{3,2,1,0:T(8,128)(2,1)} %copy.48.images, bf16[512,1536]{1,0:T(8,128)(2,1)} %all-gather.6.cloned.1.call-done.qkv_weight, ...), custom_call_target="tpu_custom_call" | custom-call | flops 109999996928 | bytes 60000000 | tf_op jit(solution)/shard_map/pallas_call | solution.py:419
  256.6 1.2 reshape.136
  257.8 0.9 fusion.5
  258.9 0.7 convert.47
  259.6 0.7 convert.49
  260.6 0.7 constant_dynamic-update-slice_fusion.8
  261.3 32.4 %reduce-scatter.8.cloned.1.call-done = bf16[128,2176]{1,0:T(8,128)(2,1)} async-done(((bf16[512,2176]{1,0:T(8,128)(2,1)}), bf16[128,2176]{1,0:T(8,128)(2,1)}) %reduce-scatter.8.cloned.1.call-update) | async-done | bytes 557072 | tf_op jit(solution)/shard_map/reduce_scatter | solution.py:311
  293.7 6.0 %copy.54 = bf16[16,14,14,512]{3,0,2,1:T(8,128)(2,1)} copy(bf16[16,14,14,512]{3,2,1,0:T(8,128)(2,1)} %get-tuple-element.76) | data formatting | bytes 6422528
  299.7 3.8 copy.55
  303.5 85.7 %all-reduce.7.cloned.1.call-done = (bf16[128,2176]{1,0:T(8,128)(2,1)}, bf16[128,2048]{1,0:T(8,128)(2,1)}, bf16[512,512]{1,0:T(8,128)(2,1)}) async-done(((bf16[128,2176]{1,0:T(8,128)(2,1)}, bf16[128,2048]{1,0:T(8,128)(2,1)}, bf16[512,512]{1,0:T(8,128)(2,1)}), (bf16[128,2176]{1,0:T(8,128)(2,1)}, bf16[128,2048]{1,0:T(8,128)(2,1)}, bf16[512,512]{1,0:T(8,128)(2,1)})) %all-reduce.7.cloned.1.call-update) | async-done | bytes 1605648 | tf_op jit(solution)/shard_map/psum | solution.py:471
  389.2 1.3 slice.120
  390.5 1.3 slice.121
  391.8 2.0 slice.122
  393.7 1.2 convert_element_type.52
  394.9 1.6 slice.124
  397.2 0.7 reshape.140
  397.8 1.1 convert_element_type.53
  398.9 1.1 convert_element_type.54
  (65 shorter events, 4.3 us)
Async XLA Ops:
  7.2 12.4 %copy-start.5 = (bf16[128,512]{1,0:T(8,128)(2,1)S(1)}, bf16[128,512]{1,0:T(8,128)(2,1)}, u32[]{:S(2)}) copy-start(bf16[128,512]{1,0:T(8,128)(2,1)} %param.19) | copy-start | bytes 393220
  7.2 24.8 %all-gather.6.cloned.1.call-start = ((), (), s32[]{:S(2)}) async-start(), calls=%async_computation.3 | async-start | bytes 1966080 | tf_op jit(solution)/shard_map/all_gather | solution.py:328
  7.9 73.5 %all-gather.10.cloned.1.call-start = ((), (), s32[]{:S(2)}) async-start(), calls=%async_computation.5 | async-start | bytes 2621440 | tf_op jit(solution)/shard_map/all_gather | solution.py:353
  16.6 15.4 %copy-start.1 = (bf16[16,14,14,512]{3,0,2,1:T(8,128)(2,1)S(1)}, bf16[16,14,14,512]{3,0,2,1:T(8,128)(2,1)}, u32[]{:S(2)}) copy-start(bf16[16,14,14,512]{3,0,2,1:T(8,128)(2,1)} %param.14) | copy-start | bytes 9633796
  32.0 51.9 %all-gather.8.cloned.1.call-start = ((), (), s32[]{:S(2)}) async-start(), calls=%async_computation.4 | async-start | bytes 3276800 | tf_op jit(solution)/shard_map/all_gather | solution.py:352
  32.0 3.6 copy-start.2
  40.1 221.2 %reduce-scatter.4.cloned.1.call-start = ((), (), s32[]{:S(2)}) async-start(), calls=%async_computation.6 | async-start | bytes 2621440 | tf_op jit(solution)/shard_map/reduce_scatter | solution.py:311
  170.6 90.6 %reduce-scatter.6.cloned.1.call-start = ((), (), s32[]{:S(2)}) async-start(), calls=%async_computation.7 | async-start | bytes 2621440 | tf_op jit(solution)/shard_map/reduce_scatter | solution.py:311
  171.2 122.5 %reduce-scatter.8.cloned.1.call-start = ((), (), s32[]{:S(2)}) async-start(), calls=%async_computation.8 | async-start | bytes 2785280 | tf_op jit(solution)/shard_map/reduce_scatter | solution.py:311
  171.5 87.3 %copy-start.7 = (f32[1,2048]{1,0:T(1,128)S(1)}, f32[1,2048]{1,0:T(1,128)}, u32[]{:S(2)}) copy-start(f32[1,2048]{1,0:T(1,128)} %get-tuple-element.49) | copy-start | bytes 24580
  171.5 88.1 %copy-start.6 = (f32[8,512]{1,0:T(8,128)S(1)}, f32[8,512]{1,0:T(8,128)}, u32[]{:S(2)}) copy-start(f32[8,512]{1,0:T(8,128)} %get-tuple-element.47) | copy-start | bytes 49156
  261.3 127.9 %all-reduce.7.cloned.1.call-start = ((), (), s32[]{:S(2)}) async-start(), calls=%async_computation.9 | async-start | bytes 3211264 | tf_op jit(solution)/shard_map/psum | solution.py:471
  293.7 6.0 %copy-start = (bf16[16,14,14,512]{3,2,1,0:T(8,128)(2,1)S(1)}, bf16[16,14,14,512]{3,2,1,0:T(8,128)(2,1)}, u32[]{:S(2)}) copy-start(bf16[16,14,14,512]{3,2,1,0:T(8,128)(2,1)} %get-tuple-element.77) | copy-start | bytes 9633796
  389.2 8.6 %copy-start.4 = (bf16[128,2048]{1,0:T(8,128)(2,1)S(1)}, bf16[128,2048]{1,0:T(8,128)(2,1)}, u32[]{:S(2)}) copy-start(bf16[128,2048]{1,0:T(8,128)(2,1)} %get-tuple-element.95) | copy-start | bytes 1572868
  393.7 5.2 %copy-start.3 = (bf16[512,512]{1,0:T(8,128)(2,1)S(1)}, bf16[512,512]{1,0:T(8,128)(2,1)}, u32[]{:S(2)}) copy-start(bf16[512,512]{1,0:T(8,128)(2,1)} %get-tuple-element.96) | copy-start | bytes 1572868
Sparse Core Ops, SparseCore 0:
  9.6 22.3 all-gather.5
  33.5 22.5 all-gather.9
  58.3 25.5 all-gather.7
  170.8 31.4 reduce-scatter.3
  204.8 31.5 reduce-scatter.5
  261.4 32.2 reduce-scatter.7
  298.0 91.1 all-reduce.6

commit v3 on v2

--- a/solution.py
+++ b/solution.py
@@ -311,8 +311,153 @@
     return lax.psum_scatter(grad, "weight", scatter_dimension=0, tiled=True)
 
 
+def owned_sum_kernel(
+    grad, other_a, other_b, out_w, out_a, out_b,
+    near_slots, near_sums, far_slot, mine, slots_w, slots_a, slots_b, work_w, work_a, work_b,
+    group_send, group_arrive, send, arrive,
+):
+    me = lax.axis_index("replica")
+    place = lax.axis_index("weight")
+
+    def bit_of(index, bit):
+        return lax.rem(index // (1 << bit), 2)
+
+    def partner(index, bit):
+        return index + (1 - 2 * bit_of(index, bit)) * (1 << bit)
+
+    barrier = pltpu.get_barrier_semaphore()
+    targets = [{"weight": partner(place, bit)} for bit in range(2)]
+    targets += [{"replica": partner(me, bit)} for bit in range(3)]
+    for target in targets:
+        pl.semaphore_signal(
+            barrier, inc=1, device_id=target, device_id_type=pl.DeviceIdType.MESH
+        )
+    pl.semaphore_wait(barrier, len(targets))
+
+    def remote(source, landing, send_sem, arrive_sem, target):
+        copy = pltpu.make_async_remote_copy(
+            src_ref=source, dst_ref=landing, send_sem=send_sem, recv_sem=arrive_sem,
+            device_id=target, device_id_type=pl.DeviceIdType.MESH,
+        )
+        copy.start()
+        return copy
+
+    height = mine.shape[0]
+
+    def shard(at):
+        return grad.at[pl.ds(pl.multiple_of(at * height, height), height)]
+
+    core, chip = bit_of(place, 0), bit_of(place, 1)
+    copies = [
+        remote(
+            shard(2 * x + 1 - core), near_slots.at[x], group_send.at[x], group_arrive.at[x], targets[0]
+        )
+        for x in range(2)
+    ]
+    for x in range(2):
+        copies[x].wait()
+        near_sums[x] = (
+            shard(2 * x + core)[...].astype(F32) + near_slots[x].astype(F32)
+        ).astype(BF16)
+    copy = remote(near_sums.at[1 - chip], far_slot, group_send.at[2], group_arrive.at[2], targets[1])
+    copy.wait()
+    mine[...] = (near_sums[chip].astype(F32) + far_slot[...].astype(F32)).astype(BF16)
+
+    sources = (mine, other_a, other_b)
+    outs = (out_w, out_a, out_b)
+    slots = (slots_w, slots_a, slots_b)
+    works = (work_w, work_a, work_b)
+    orders = ((0, 1, 2), (1, 0, 2))
+    bases = []
+    for order in orders:
+        base = [0 * me]
+        for s, bit in enumerate(order):
+            base.append(base[-1] + bit_of(me, bit) * (4 >> s))
+        bases.append(base)
+
+    def block(ref, half, first, chunks):
+        size = ref.shape[0] // 8
+        columns = (ref.shape[1] // 256) * 128
+        rows = pl.ds(pl.multiple_of(first * size, size), chunks * size)
+        if half == 0:
+            return ref.at[rows, :columns]
+        return ref.at[rows, columns:]
+
+    def start_sum(s, half):
+        bit = orders[half][s]
+        chunks = 4 >> s
+        away = bases[half][s] + (1 - bit_of(me, bit)) * chunks
+        begin = sum(4 >> k for k in range(s))
+        return [
+            remote(
+                block(sources[a] if s == 0 else works[a], half, away, chunks),
+                block(slots[a], half, begin, chunks),
+                send.at[0, s, half, a], arrive.at[0, s, half, a], targets[2 + bit],
+            )
+            for a in range(3)
+        ]
+
+    def end_sum(s, half, copies):
+        chunks = 4 >> s
+        begin = sum(4 >> k for k in range(s))
+        for a in range(3):
+            copies[a].wait()
+            held = block(sources[a] if s == 0 else works[a], half, bases[half][s + 1], chunks)
+            total = held[...].astype(F32) + block(slots[a], half, begin, chunks)[...].astype(F32)
+            kept_in = outs[a] if s == 2 else works[a]
+            block(kept_in, half, bases[half][s + 1], chunks)[...] = total.astype(BF16)
+
+    def start_share(s, half):
+        bit = orders[half][s]
+        chunks = 4 >> s
+        return [
+            remote(
+                block(outs[a], half, bases[half][s + 1], chunks),
+                block(outs[a], half, bases[half][s + 1], chunks),
+                send.at[1, s, half, a], arrive.at[1, s, half, a], targets[2 + bit],
+            )
+            for a in range(3)
+        ]
+
+    flying = [start_sum(0, 0), start_sum(0, 1)]
+    for s in range(3):
+        for half in range(2):
+            end_sum(s, half, flying[half])
+            flying[half] = start_sum(s + 1, half) if s < 2 else start_share(2, half)
+    for s in (2, 1, 0):
+        for half in range(2):
+            for copy in flying[half]:
+                copy.wait()
+            if s > 0:
+                flying[half] = start_share(s - 1, half)
+
+
+def owned_sums(grad, others, shards, replicas):
+    if shards != 4 or replicas != 8:
+        return lax.psum((reduce_owned(grad),) + others, "replica")
+    height = grad.shape[0] // shards
+    shapes = [(height, grad.shape[1])] + [other.shape for other in others]
+    vmem = pl.BlockSpec(memory_space=pltpu.VMEM)
+    return pl.pallas_call(
+        owned_sum_kernel,
+        in_specs=[vmem] * 3,
+        out_specs=[vmem] * 3,
+        out_shape=[jax.ShapeDtypeStruct(shape, BF16) for shape in shapes],
+        scratch_shapes=[
+            pltpu.VMEM((2,) + shapes[0], BF16), pltpu.VMEM((2,) + shapes[0], BF16),
+            pltpu.VMEM(shapes[0], BF16), pltpu.VMEM(shapes[0], BF16),
+        ]
+        + [pltpu.VMEM(shape, BF16) for shape in shapes] * 2
+        + [pltpu.SemaphoreType.DMA((3,))] * 2
+        + [pltpu.SemaphoreType.DMA((2, 3, 2, 3))] * 2,
+        compiler_params=pltpu.CompilerParams(
+            collective_id=0, has_side_effects=True, vmem_limit_bytes=32 * 1024 * 1024
+        ),
+    )(grad, *others)
+
+
 def per_device(
-    shards, images, gains, biases, qkv_weight, bias_table, proj_weight, fc1_weight, fc1_bias,
+    shards, replicas, images, gains, biases, qkv_weight, bias_table, proj_weight, fc1_weight, fc1_bias,
     fc2_weight, rel_index, cotangent,
 ):
     number, width = images.shape[0], images.shape[-1]
@@ -468,8 +613,8 @@
     weight_grad, expand_owned, reduce_owned_grad = lax.optimization_barrier(
         (weight_grad, expand_owned, reduce_owned_grad)
     )
-    weight_owned, expand_owned, reduce_owned_grad = lax.psum(
-        (reduce_owned(weight_grad), expand_owned, reduce_owned_grad), "replica"
+    weight_owned, expand_owned, reduce_owned_grad = owned_sums(
+        weight_grad, (expand_owned, reduce_owned_grad), shards, replicas
     )
     weight_owned = weight_owned.astype(F32)
     small_owned = weight_owned[:, 4 * width :]
@@ -516,7 +661,7 @@
         P("weight", None),
     )
     return jax.shard_map(
-        functools.partial(per_device, mesh.shape["weight"]),
+        functools.partial(per_device, mesh.shape["weight"], mesh.shape["replica"]),
         mesh=mesh,
         in_specs=in_specs,
         out_specs=out_specs,

time: 407 us -> 349 us (0.86)
  waiting for transfers between devices: 132 us -> 13.9 us
  Pallas kernels: 213 us -> 281 us
  local copies, waits for them, and re-layouts: 30.2 us -> 25.1 us
    psum x1 -> x0, waiting for transfers between devices: 85.7 us -> none  [per_device(): lax.psum((reduce_owned(weight_grad), expand_owned, reduce_owned_grad), 'r...]
    pallas_call x0 -> x1, Pallas kernels: none -> 68.1 us  [owned_sums(): pl.pallas_call(owned_sum_kernel, in_specs=[vmem] * 3, out_specs=[vmem] *...]
    reduce_scatter x3 -> x2, waiting for transfers between devices: 32.4 us -> 0.04 us  [reduce_owned(): return lax.psum_scatter(grad, 'weight', scatter_dimension=0, tiled=True)]
    unnamed x31 -> x33, local copies, waits for them, and re-layouts: 17.5 us -> 17.3 us
  transfers between devices with their start and end apart: 7 -> 5, of which waited for: 4 -> 2; matrix products, arithmetic and copies ran while one was open for 7% -> 7% of each run, Pallas kernels for 31% -> 36%
where the time goes in v3:
time: 349 us
  Pallas kernels  281 us (81%)
  local copies, waits for them, and re-layouts  25.1 us (7%)
  between operations  14 us (4%)
  waiting for transfers between devices  13.9 us (4%)
  other arithmetic  6.21 us (2%)
  blocking collectives  6.19 us (2%)
    pallas_call x1, Pallas kernels, per_device(): pl.pallas_call(mlp_kernel, grid=(steps,), in_specs=[image_block, image_bl...  86.8 us
    pallas_call x1, Pallas kernels, per_device(): pl.pallas_call(functools.partial(backward_kernel, width_head), grid=(step...  85.2 us
    pallas_call x1, Pallas kernels, owned_sums(): pl.pallas_call(owned_sum_kernel, in_specs=[vmem] * 3, out_specs=[vmem] *...  68.1 us
    pallas_call x1, Pallas kernels, per_device(): pl.pallas_call(functools.partial(attention_kernel, width_head), grid=(ste...  41.1 us
    unnamed x33, local copies, waits for them, and re-layouts  17.3 us
    all_gather x1, waiting for transfers between devices, per_device(): qkv_full = lax.all_gather(qkv_weight, 'weight', axis=0, tiled=True)  10.5 us
  transfers between devices with their start and end apart: 5, of which 2 were waited for; matrix products, arithmetic and copies ran while one was open for 7% of the time, Pallas kernels for 36%

profile of v3, /device:TPU:0, one launch (start us, length us, event | category | flops | bytes accessed | tf_op | source)
XLA Modules:
  0.0 348.9 jit_solution(1814997373915478858)
XLA Ops:
  7.2 0.7 all-gather.6.cloned.1.call-update
  8.0 0.8 reshape.129
  8.7 0.7 maximum_bitcast_fusion
  9.5 6.2 %all-gather.1 = bf16[4,18,128]{2,1,0:T(8,128)(2,1)S(1)} all-gather(bf16[1,18,128]{2,1,0:T(8,128)(2,1)S(1)} %maximum_bitcast_fusion), channel_id=2, replica_groups=mesh['replica'=8,'weight'=4] {'weight'}, dimensions={0}, use_global_device_ids=true | all-gather | bytes 23040 | tf_op jit(solution)/shard_map/all_gather | solution.py:481
  15.8 0.8 copy.57
  16.6 0.8 fusion.1
  17.5 0.8 pad.19.clone
  18.3 0.6 slice_convert_fusion
  18.9 0.6 convert_bitcast_fusion.1
  19.5 2.0 pad_maximum_fusion
  21.5 10.5 %all-gather.6.cloned.1.call-done.qkv_weight = bf16[512,1536]{1,0:T(8,128)(2,1)} async-done(((bf16[128,1536]{1,0:T(8,128)(2,1)}), bf16[512,1536]{1,0:T(8,128)(2,1)}) %all-gather.6.cloned.1.call-update) | async-done | bytes 1572880 | tf_op jit(solution)/shard_map/all_gather | solution.py:473
  32.1 3.6 %copy.60.images = bf16[16,14,14,512]{3,2,1,0:T(8,128)(2,1)} copy(bf16[16,14,14,512]{3,0,2,1:T(8,128)(2,1)S(1)} %copy-done.5) | data formatting | bytes 6422528 | tf_op args[0]
  35.7 3.8 %copy.61.cotangent = bf16[16,14,14,512]{3,2,1,0:T(8,128)(2,1)} copy(bf16[16,14,14,512]{3,0,2,1:T(8,128)(2,1)S(1)} %copy-done.6) | data formatting | bytes 6422528 | tf_op args[10]
  39.5 0.6 broadcast_in_dim.8.qkv_bias
  40.3 41.1 %shard_map.213 = (bf16[3584,1536]{1,0:T(8,128)(2,1)}, bf16[3584,512]{1,0:T(8,128)(2,1)}, bf16[256,224,56]{2,1,0:T(8,128)(2,1)}) custom-call(bf16[16,14,14,512]{3,2,1,0:T(8,128)(2,1)} %copy.60.images, bf16[512,1536]{1,0:T(8,128)(2,1)} %all-gather.6.cloned.1.call-done.qkv_weight, f32[8,512]{1,0:T(8,128)} %get-tuple-element.37.vectors, ...), custom_call_target="tpu_custom_call" | custom-call | flops 60000002048 | bytes 40000000 | tf_op jit(solution)/shard_map/pallas_call | solution.py:510
  81.4 2.5 all-gather.8.cloned.1.call-done.later.proj_weight
  83.9 86.8 %shard_map.214 = (bf16[16,14,14,512]{3,2,1,0:T(8,128)(2,1)}, f32[3584,512]{1,0:T(8,128)}, bf16[512,2048]{1,0:T(8,128)(2,1)}, bf16[2048,512]{1,0:T(8,128)(2,1)}, f32[8,512]{1,0:T(8,128)}, /*index=5*/f32[1,2048]{1,0:T(1,128)}) custom-call(bf16[16,14,14,512]{3,2,1,0:T(8,128)(2,1)} %copy.60.images, bf16[16,14,14,512]{3,2,1,0:T(8,128)(2,1)} %copy.61.cotangent, ...), custom_call_target="tpu_custom_call" | custom-call | flops 70000001024 | bytes 40000000 | tf_op jit(solution)/shard_map/pallas_call | solution.py:533
  171.3 85.2 %shard_map.215 = (bf16[16,14,14,512]{3,2,1,0:T(8,128)(2,1)}, bf16[512,2176]{1,0:T(8,128)(2,1)}, f32[8,512]{1,0:T(8,128)}, f32[1,1536]{1,0:T(1,128)}, f32[4,224,56]{2,1,0:T(8,128)}) custom-call(bf16[16,14,14,512]{3,2,1,0:T(8,128)(2,1)} %copy.60.images, bf16[512,1536]{1,0:T(8,128)(2,1)} %all-gather.6.cloned.1.call-done.qkv_weight, ...), custom_call_target="tpu_custom_call" | custom-call | flops 109999996928 | bytes 60000000 | tf_op jit(solution)/shard_map/pallas_call | solution.py:564
  256.6 3.8 %copy.72 = bf16[16,14,14,512]{3,0,2,1:T(8,128)(2,1)} copy(bf16[16,14,14,512]{3,2,1,0:T(8,128)(2,1)S(1)} %copy-done.3) | data formatting | bytes 6422528
  260.4 3.8 %copy.73 = bf16[16,14,14,512]{3,0,2,1:T(8,128)(2,1)} copy(bf16[16,14,14,512]{3,2,1,0:T(8,128)(2,1)S(1)} %copy-done.4) | data formatting | bytes 6422528
  264.5 0.9 fusion.5
  265.8 1.0 copy-done.1
  266.9 1.0 copy-done.2
  267.9 68.1 %shard_map.216 = (bf16[128,2176]{1,0:T(8,128)(2,1)S(1)}, bf16[128,2048]{1,0:T(8,128)(2,1)S(1)}, bf16[512,512]{1,0:T(8,128)(2,1)S(1)}) custom-call(bf16[512,2176]{1,0:T(8,128)(2,1)S(1)} %constant_dynamic-update-slice_fusion.grad, bf16[128,2048]{1,0:T(8,128)(2,1)S(1)} %copy-done.1, bf16[512,512]{1,0:T(8,128)(2,1)S(1)} %copy-done.2), custom_call_target="tpu_custom_call" | custom-call | tf_op jit(solution)/shard_map/pallas_call | solution.py:441
  336.1 0.6 slice.120
  336.6 0.6 slice.121
  337.2 1.0 slice.122
  338.2 0.7 slice.124
  339.0 0.6 slice_bitcast_fusion.2
  339.6 0.7 reshape.140
  340.2 1.1 convert_element_type.53
  341.3 1.1 convert_element_type.54
  (60 shorter events, 1.9 us)
Async XLA Ops:
  7.2 12.4 %copy-start.8 = (bf16[128,512]{1,0:T(8,128)(2,1)S(1)}, bf16[128,512]{1,0:T(8,128)(2,1)}, u32[]{:S(2)}) copy-start(bf16[128,512]{1,0:T(8,128)(2,1)} %param.19) | copy-start | bytes 393220
  7.2 24.8 %all-gather.6.cloned.1.call-start = ((), (), s32[]{:S(2)}) async-start(), calls=%async_computation.2 | async-start | bytes 1966080 | tf_op jit(solution)/shard_map/all_gather | solution.py:473
  7.9 73.5 %all-gather.10.cloned.1.call-start = ((), (), s32[]{:S(2)}) async-start(), calls=%async_computation.4 | async-start | bytes 2621440 | tf_op jit(solution)/shard_map/all_gather | solution.py:498
  16.6 15.4 %copy-start.5 = (bf16[16,14,14,512]{3,0,2,1:T(8,128)(2,1)S(1)}, bf16[16,14,14,512]{3,0,2,1:T(8,128)(2,1)}, u32[]{:S(2)}) copy-start(bf16[16,14,14,512]{3,0,2,1:T(8,128)(2,1)} %param.14) | copy-start | bytes 9633796
  32.0 51.9 %all-gather.8.cloned.1.call-start = ((), (), s32[]{:S(2)}) async-start(), calls=%async_computation.3 | async-start | bytes 3276800 | tf_op jit(solution)/shard_map/all_gather | solution.py:497
  32.0 3.6 %copy-start.6 = (bf16[16,14,14,512]{3,0,2,1:T(8,128)(2,1)S(1)}, bf16[16,14,14,512]{3,0,2,1:T(8,128)(2,1)}, u32[]{:S(2)}) copy-start(bf16[16,14,14,512]{3,0,2,1:T(8,128)(2,1)} %param.24) | copy-start | bytes 9633796
  40.1 225.7 %reduce-scatter.3.cloned.1.call-start = ((), (), s32[]{:S(2)}) async-start(), calls=%async_computation.5 | async-start | bytes 2621440 | tf_op jit(solution)/shard_map/reduce_scatter | solution.py:311
  170.7 95.1 %reduce-scatter.5.cloned.1.call-start = ((), (), s32[]{:S(2)}) async-start(), calls=%async_computation.6 | async-start | bytes 2621440 | tf_op jit(solution)/shard_map/reduce_scatter | solution.py:311
  171.3 85.3 %copy-start.3 = (bf16[16,14,14,512]{3,2,1,0:T(8,128)(2,1)S(1)}, bf16[16,14,14,512]{3,2,1,0:T(8,128)(2,1)}, u32[]{:S(2)}) copy-start(bf16[16,14,14,512]{3,2,1,0:T(8,128)(2,1)} %get-tuple-element.82) | copy-start | bytes 9633796
  256.6 3.9 %copy-start.4 = (bf16[16,14,14,512]{3,2,1,0:T(8,128)(2,1)S(1)}, bf16[16,14,14,512]{3,2,1,0:T(8,128)(2,1)}, u32[]{:S(2)}) copy-start(bf16[16,14,14,512]{3,2,1,0:T(8,128)(2,1)} %get-tuple-element.83) | copy-start | bytes 9633796
  260.4 3.9 %copy-start.7 = (f32[4,224,56]{2,1,0:T(8,128)S(1)}, f32[4,224,56]{2,1,0:T(8,128)}, u32[]{:S(2)}) copy-start(f32[4,224,56]{2,1,0:T(8,128)} %get-tuple-element.53) | copy-start | bytes 602116
  260.4 5.1 %copy-start.9 = (f32[8,512]{1,0:T(8,128)S(1)}, f32[8,512]{1,0:T(8,128)}, u32[]{:S(2)}) copy-start(f32[8,512]{1,0:T(8,128)} %get-tuple-element.50) | copy-start | bytes 49156
  260.4 5.1 %copy-start.10 = (f32[8,512]{1,0:T(8,128)S(1)}, f32[8,512]{1,0:T(8,128)}, u32[]{:S(2)}) copy-start(f32[8,512]{1,0:T(8,128)} %get-tuple-element.49) | copy-start | bytes 49156
  260.4 5.1 %copy-start.12 = (f32[1,1536]{1,0:T(1,128)S(1)}, f32[1,1536]{1,0:T(1,128)}, u32[]{:S(2)}) copy-start(f32[1,1536]{1,0:T(1,128)} %get-tuple-element.51) | copy-start | bytes 18436
  260.4 5.2 %copy-start.11 = (f32[1,2048]{1,0:T(1,128)S(1)}, f32[1,2048]{1,0:T(1,128)}, u32[]{:S(2)}) copy-start(f32[1,2048]{1,0:T(1,128)} %get-tuple-element.52) | copy-start | bytes 24580
  260.4 5.3 %copy-start = (bf16[512,2176]{1,0:T(8,128)(2,1)S(1)}, bf16[512,2176]{1,0:T(8,128)(2,1)}, u32[]{:S(2)}) copy-start(bf16[512,2176]{1,0:T(8,128)(2,1)} %get-tuple-element.48) | copy-start | bytes 6684676
  265.8 1.0 copy-start.1
  266.9 1.0 copy-start.2
Sparse Core Ops, SparseCore 0:
  9.6 22.3 all-gather.5
  33.5 22.5 all-gather.9
  58.3 25.5 all-gather.7
  170.8 31.4 reduce-scatter.2
  204.8 31.4 reduce-scatter.4
